TPU v7x, 32 devices: a whole 2x2x4 slice. The times are simulated.
32 devices in a mesh: seq: 2 (over y), chain: 16 (over z, x, core).
Axes of the slice: x: 2, y: 2, z: 4, core: 2. Of those that a mesh axis runs over, the one named last changes fastest.
Arguments:
- tokens: bfloat16 [16, 2, 512, 768], P('chain', None, 'seq'), may hold values from -6 to 6
- cotangent: bfloat16 [16, 2, 512, 768], P('chain', None, 'seq'), may hold values from -6 to 6
- chain_start: int32 [16, 2], P('chain'), may hold values from 0 to 1, as said below
- seg_len: int32 [16, 2], P('chain'), may hold values from 1 to 512, as said below
- query_weight: bfloat16 [768, 768], P(('seq', 'chain')), may hold values from -0.21875 to 0.21875
- key_weight: bfloat16 [768, 768], P(('seq', 'chain')), may hold values from -0.21875 to 0.21875
- value_weight: bfloat16 [768, 768], P(('seq', 'chain')), may hold values from -0.21875 to 0.21875
- output_weight: bfloat16 [768, 768], P(('seq', 'chain')), may hold values from -0.625 to 0.625
- query_bias: bfloat16 [768], P(('seq', 'chain')), may hold values from -1.796875 to 1.796875
- value_bias: bfloat16 [768], P(('seq', 'chain')), may hold values from -1.796875 to 1.796875
- output_bias: bfloat16 [768], P(('seq', 'chain')), may hold values from -1.796875 to 1.796875
- first_gain: bfloat16 [768], P(('seq', 'chain')), may hold values from 0.5 to 1.5
- first_shift: bfloat16 [768], P(('seq', 'chain')), may hold values from -1.796875 to 1.796875
- inner_weight: bfloat16 [768, 3072], P(('seq', 'chain')), may hold values from -0.21875 to 0.21875
- inner_bias: bfloat16 [3072], P(('seq', 'chain')), may hold values from -1.796875 to 1.796875
- outer_weight: bfloat16 [3072, 768], P(('seq', 'chain')), may hold values from -0.109375 to 0.109375
- outer_bias: bfloat16 [768], P(('seq', 'chain')), may hold values from -1.796875 to 1.796875
- second_gain: bfloat16 [768], P(('seq', 'chain')), may hold values from 0.5 to 1.5
- second_shift: bfloat16 [768], P(('seq', 'chain')), may hold values from -1.796875 to 1.796875
- read_init: bfloat16 [10, 768], P(None, ('seq', 'chain')), may hold values from -6 to 6
- write_init: bfloat16 [10, 768], P(None, ('seq', 'chain')), may hold values from -6 to 6
Outputs:
- layer_out: bfloat16 [16, 2, 512, 768], P('chain', None, 'seq')
- input_grad: bfloat16 [16, 2, 512, 768], P('chain', None, 'seq')
- query_weight_grad: float32 [768, 768], P(('seq', 'chain'))
- key_weight_grad: float32 [768, 768], P(('seq', 'chain'))
- value_weight_grad: float32 [768, 768], P(('seq', 'chain'))
- output_weight_grad: float32 [768, 768], P(('seq', 'chain'))
- query_bias_grad: float32 [768], P(('seq', 'chain'))
- value_bias_grad: float32 [768], P(('seq', 'chain'))
- output_bias_grad: float32 [768], P(('seq', 'chain'))
- first_gain_grad: float32 [768], P(('seq', 'chain'))
- first_shift_grad: float32 [768], P(('seq', 'chain'))
- inner_weight_grad: float32 [768, 3072], P(('seq', 'chain'))
- inner_bias_grad: float32 [3072], P(('seq', 'chain'))
- outer_weight_grad: float32 [3072, 768], P(('seq', 'chain'))
- outer_bias_grad: float32 [768], P(('seq', 'chain'))
- second_gain_grad: float32 [768], P(('seq', 'chain'))
- second_shift_grad: float32 [768], P(('seq', 'chain'))
- read_init_grad: float32 [10, 768], P(None, ('seq', 'chain'))
- write_init_grad: float32 [10, 768], P(None, ('seq', 'chain'))
Inputs may be any that keep to these rules, and one draw needn't show every extreme that they name: `chain_start`: every group's first slot begins a chain; a chain holds one to 2 consecutive slots of one group. `seg_len`: A segment that its document continues past (the next slot has chain_start 0) is full; only a chain's last segment may be partial.
All inputs are finite; a program needn't handle non-finite values.
Results may differ from a plain program's by a relative error of at most 0.018.
Values may be sent and summed in bfloat16 or wider, within the bound.
A program may use at most 192 MiB of HBM per device.

v0:
```python
import math

import jax
import jax.numpy as jnp
from jax import lax
from jax.sharding import PartitionSpec as P

HEADS = 12
MEM = 10


EPS = 1e-12
INV_ROOT_TWO = 1.0 / math.sqrt(2.0)
INV_ROOT_TWO_PI = 1.0 / math.sqrt(2.0 * math.pi)
NEG_FILL = -1000000000.0


def matmul(former, latter):
    return jnp.dot(former, latter, preferred_element_type=jnp.float32)


def matmul_tn(former, latter):
    return lax.dot_general(
        former, latter, (((0,), (0,)), ((), ())), preferred_element_type=jnp.float32
    )


def matmul_nt(former, latter):
    return lax.dot_general(
        former, latter, (((1,), (1,)), ((), ())), preferred_element_type=jnp.float32
    )


def norm_keep(summed, gain_vec, shift_vec):
    row_mean = jnp.mean(summed, axis=-1, keepdims=True)
    centred = summed - row_mean
    inverse = lax.rsqrt(jnp.mean(centred * centred, axis=-1, keepdims=True) + EPS)
    normed = centred * inverse
    return (normed * gain_vec + shift_vec, normed, inverse)


def norm_back(grad_out, gain_vec, normed, inverse):
    scaled = grad_out * gain_vec
    return inverse * (
        scaled
        - jnp.mean(scaled, axis=-1, keepdims=True)
        - normed * jnp.mean(scaled * normed, axis=-1, keepdims=True)
    )


def gelu_parts(inner_pre):
    cumulative = 0.5 * (1.0 + lax.erf(inner_pre * INV_ROOT_TWO))
    density = jnp.exp(-0.5 * inner_pre * inner_pre) * INV_ROOT_TWO_PI
    return (inner_pre * cumulative, cumulative + inner_pre * density)


def score_rows(query_heads, key_heads, key_valid, score_scale):
    raw_scores = jnp.einsum(
        "qhd,khd->hqk", query_heads, key_heads, preferred_element_type=jnp.float32
    )
    return jnp.where(key_valid[None, None, :], raw_scores * score_scale, NEG_FILL)


def column_sum(values_in):
    return jnp.sum(values_in.astype(jnp.float32), axis=0)


def stacked(items, place):
    return jnp.concatenate([entry[place] for entry in items], axis=0)


def shards(
    tokens,
    cotangent,
    chain_start,
    seg_len,
    query_weight,
    key_weight,
    value_weight,
    output_weight,
    query_bias,
    value_bias,
    output_bias,
    first_gain,
    first_shift,
    inner_weight,
    inner_bias,
    outer_weight,
    outer_bias,
    second_gain,
    second_shift,
    read_init,
    write_init,
):
    whole = (
        lax.all_gather(query_weight, ("seq", "chain"), axis=0, tiled=True),
        lax.all_gather(key_weight, ("seq", "chain"), axis=0, tiled=True),
        lax.all_gather(value_weight, ("seq", "chain"), axis=0, tiled=True),
        lax.all_gather(output_weight, ("seq", "chain"), axis=0, tiled=True),
        lax.all_gather(query_bias, ("seq", "chain"), axis=0, tiled=True),
        lax.all_gather(value_bias, ("seq", "chain"), axis=0, tiled=True),
        lax.all_gather(output_bias, ("seq", "chain"), axis=0, tiled=True),
        lax.all_gather(first_gain, ("seq", "chain"), axis=0, tiled=True),
        lax.all_gather(first_shift, ("seq", "chain"), axis=0, tiled=True),
        lax.all_gather(inner_weight, ("seq", "chain"), axis=0, tiled=True),
        lax.all_gather(inner_bias, ("seq", "chain"), axis=0, tiled=True),
        lax.all_gather(outer_weight, ("seq", "chain"), axis=0, tiled=True),
        lax.all_gather(outer_bias, ("seq", "chain"), axis=0, tiled=True),
        lax.all_gather(second_gain, ("seq", "chain"), axis=0, tiled=True),
        lax.all_gather(second_shift, ("seq", "chain"), axis=0, tiled=True),
        lax.all_gather(read_init, ("seq", "chain"), axis=1, tiled=True),
        lax.all_gather(write_init, ("seq", "chain"), axis=1, tiled=True),
    )
    (
        whole_query,
        whole_key,
        whole_value,
        whole_output,
        bias_query,
        bias_value,
        bias_output,
        gain_one,
        shift_one,
        whole_inner,
        bias_inner,
        whole_outer,
        bias_outer,
        gain_two,
        shift_two,
        read_b,
        write_b,
    ) = whole
    bias_query_f = bias_query.astype(jnp.float32)
    bias_value_f = bias_value.astype(jnp.float32)
    bias_output_f = bias_output.astype(jnp.float32)
    gain_one_f = gain_one.astype(jnp.float32)
    shift_one_f = shift_one.astype(jnp.float32)
    bias_inner_f = bias_inner.astype(jnp.float32)
    bias_outer_f = bias_outer.astype(jnp.float32)
    gain_two_f = gain_two.astype(jnp.float32)
    shift_two_f = shift_two.astype(jnp.float32)
    slot_count = tokens.shape[1]
    half_rows = tokens.shape[2]
    model_width = tokens.shape[3]
    head_count = HEADS
    head_size = model_width // head_count
    score_scale = 1.0 / math.sqrt(head_size)
    local_rows = 2 * MEM + half_rows
    pair_size = lax.axis_size("seq")
    my_index = lax.axis_index("seq")
    key_index = jnp.arange(pair_size * local_rows)
    source = key_index // local_rows
    within = key_index % local_rows
    carried = jnp.zeros((MEM, model_width), jnp.bfloat16)
    saved = []
    outputs = []
    for slot_index in range(slot_count):
        owner_index = slot_index % pair_size
        length = seg_len[0, slot_index]
        read_rows = jnp.where(chain_start[0, slot_index] == 1, read_b, carried)
        hidden = jnp.concatenate([read_rows, write_b, tokens[0, slot_index]], axis=0)
        query_val = (matmul(hidden, whole_query) + bias_query_f).astype(jnp.bfloat16)
        key_val = matmul(hidden, whole_key).astype(jnp.bfloat16)
        value_val = (matmul(hidden, whole_value) + bias_value_f).astype(jnp.bfloat16)
        all_keys, all_values = (
            lax.all_gather(key_val, "seq", axis=0, tiled=True),
            lax.all_gather(value_val, "seq", axis=0, tiled=True),
        )
        key_valid = jnp.where(
            within < 2 * MEM, source == owner_index, source * half_rows + within - 2 * MEM < length
        )
        query_heads = query_val.reshape(local_rows, head_count, head_size)
        key_heads = all_keys.reshape(pair_size * local_rows, head_count, head_size)
        value_heads = all_values.reshape(pair_size * local_rows, head_count, head_size)
        scores = score_rows(query_heads, key_heads, key_valid, score_scale)
        row_max = jnp.max(scores, axis=-1, keepdims=True)
        row_total = jnp.sum(jnp.exp(scores - row_max), axis=-1, keepdims=True)
        log_total = row_max + jnp.log(row_total)
        probs_b = jnp.exp(scores - log_total).astype(jnp.bfloat16)
        mixed_out = jnp.einsum(
            "hqk,khd->qhd", probs_b, value_heads, preferred_element_type=jnp.float32
        )
        mixed_b = mixed_out.reshape(local_rows, model_width).astype(jnp.bfloat16)
        branch = matmul(mixed_b, whole_output) + bias_output_f
        first, normed_one, inverse_one = norm_keep(
            hidden.astype(jnp.float32) + branch, gain_one_f, shift_one_f
        )
        first_b = first.astype(jnp.bfloat16)
        inner_pre = matmul(first_b, whole_inner) + bias_inner_f
        active, gelu_slope = gelu_parts(inner_pre)
        active_b = active.astype(jnp.bfloat16)
        outer = matmul(active_b, whole_outer) + bias_outer_f
        second, normed_two, inverse_two = norm_keep(first + outer, gain_two_f, shift_two_f)
        outputs.append(second[2 * MEM :].astype(jnp.bfloat16))
        carried = second[MEM : 2 * MEM].astype(jnp.bfloat16)
        saved.append(
            (
                hidden,
                query_heads,
                key_heads,
                value_heads,
                key_valid,
                log_total,
                mixed_b,
                normed_one,
                inverse_one,
                first_b,
                gelu_slope,
                active_b,
                normed_two,
                inverse_two,
            )
        )
    layer_out = jnp.stack(outputs, axis=0)[None]
    grad_list = [jnp.zeros(w.shape, jnp.float32) for w in whole]
    carry_grad = jnp.zeros((MEM, model_width), jnp.float32)
    input_list = [None] * slot_count
    product_terms = []
    for slot_index in reversed(range(slot_count)):
        owner_index = slot_index % pair_size
        is_owner = my_index == owner_index
        (
            hidden,
            query_heads,
            key_heads,
            value_heads,
            key_valid,
            log_total,
            mixed_b,
            normed_one,
            inverse_one,
            first_b,
            gelu_slope,
            active_b,
            normed_two,
            inverse_two,
        ) = saved[slot_index]
        write_part = jnp.where(is_owner, carry_grad, 0.0)
        grad_out = jnp.concatenate(
            [
                jnp.zeros((MEM, model_width), jnp.float32),
                write_part,
                cotangent[0, slot_index].astype(jnp.float32),
            ],
            axis=0,
        )
        grad_list[13] = grad_list[13] + jnp.sum(grad_out * normed_two, axis=0)
        grad_list[14] = grad_list[14] + jnp.sum(grad_out, axis=0)
        grad_two = norm_back(grad_out, gain_two_f, normed_two, inverse_two)
        grad_two_b = grad_two.astype(jnp.bfloat16)
        grad_list[12] = grad_list[12] + column_sum(grad_two_b)
        grad_inner_b = (matmul_nt(grad_two_b, whole_outer) * gelu_slope).astype(jnp.bfloat16)
        grad_list[10] = grad_list[10] + column_sum(grad_inner_b)
        grad_first = matmul_nt(grad_inner_b, whole_inner) + grad_two
        grad_list[7] = grad_list[7] + jnp.sum(grad_first * normed_one, axis=0)
        grad_list[8] = grad_list[8] + jnp.sum(grad_first, axis=0)
        grad_one = norm_back(grad_first, gain_one_f, normed_one, inverse_one)
        grad_one_b = grad_one.astype(jnp.bfloat16)
        grad_list[6] = grad_list[6] + column_sum(grad_one_b)
        grad_mixed = matmul_nt(grad_one_b, whole_output).astype(jnp.bfloat16)
        grad_mixed_heads = grad_mixed.reshape(local_rows, head_count, head_size)
        scores = score_rows(query_heads, key_heads, key_valid, score_scale)
        probs = jnp.exp(scores - log_total)
        probs_b = probs.astype(jnp.bfloat16)
        grad_probs = jnp.einsum(
            "qhd,khd->hqk", grad_mixed_heads, value_heads, preferred_element_type=jnp.float32
        )
        row_delta = jnp.sum(grad_probs * probs, axis=-1, keepdims=True)
        grad_scores_b = (probs * (grad_probs - row_delta)).astype(jnp.bfloat16)
        grad_query = (
            jnp.einsum("hqk,khd->qhd", grad_scores_b, key_heads, preferred_element_type=jnp.float32)
            * score_scale
        )
        key_terms = (
            jnp.einsum(
                "hqk,qhd->khd", grad_scores_b, query_heads, preferred_element_type=jnp.float32
            )
            * score_scale
        )
        value_terms = jnp.einsum(
            "hqk,qhd->khd", probs_b, grad_mixed_heads, preferred_element_type=jnp.float32
        )
        grad_keys, grad_values = (
            lax.psum_scatter(
                key_terms.reshape(pair_size * local_rows, model_width).astype(jnp.bfloat16),
                "seq",
                scatter_dimension=0,
                tiled=True,
            ).astype(jnp.float32),
            lax.psum_scatter(
                value_terms.reshape(pair_size * local_rows, model_width).astype(jnp.bfloat16),
                "seq",
                scatter_dimension=0,
                tiled=True,
            ).astype(jnp.float32),
        )
        grad_query_b = grad_query.reshape(local_rows, model_width).astype(jnp.bfloat16)
        grad_keys_b = grad_keys.astype(jnp.bfloat16)
        grad_values_b = grad_values.astype(jnp.bfloat16)
        grad_list[4] = grad_list[4] + column_sum(grad_query_b)
        grad_list[5] = grad_list[5] + column_sum(grad_values_b)
        product_terms.append(
            (
                hidden,
                grad_query_b,
                grad_keys_b,
                grad_values_b,
                mixed_b,
                grad_one_b,
                first_b,
                grad_inner_b,
                active_b,
                grad_two_b,
            )
        )
        grad_hidden = (
            matmul_nt(grad_query_b, whole_query)
            + matmul_nt(grad_keys_b, whole_key)
            + matmul_nt(grad_values_b, whole_value)
            + grad_one
        )
        input_list[slot_index] = grad_hidden[2 * MEM :].astype(jnp.bfloat16)
        read_grad = jnp.where(is_owner, grad_hidden[:MEM], 0.0)
        grad_list[16] = grad_list[16] + jnp.where(is_owner, grad_hidden[MEM : 2 * MEM], 0.0)
        restart = chain_start[0, slot_index] == 1
        grad_list[15] = grad_list[15] + jnp.where(restart, read_grad, 0.0)
        if slot_index > 0:
            carry_grad = lax.psum(jnp.where(restart, 0.0, read_grad), "seq")
    input_grad = jnp.stack(input_list, axis=0)[None]
    all_hidden = stacked(product_terms, 0)
    grad_list[0] = matmul_tn(all_hidden, stacked(product_terms, 1))
    grad_list[1] = matmul_tn(all_hidden, stacked(product_terms, 2))
    grad_list[2] = matmul_tn(all_hidden, stacked(product_terms, 3))
    grad_list[3] = matmul_tn(stacked(product_terms, 4), stacked(product_terms, 5))
    grad_list[9] = matmul_tn(stacked(product_terms, 6), stacked(product_terms, 7))
    grad_list[11] = matmul_tn(stacked(product_terms, 8), stacked(product_terms, 9))
    within_group = (
        lax.psum_scatter(
            grad_list[0].astype(jnp.bfloat16), "seq", scatter_dimension=0, tiled=True
        ).astype(jnp.float32),
        lax.psum_scatter(
            grad_list[1].astype(jnp.bfloat16), "seq", scatter_dimension=0, tiled=True
        ).astype(jnp.float32),
        lax.psum_scatter(
            grad_list[2].astype(jnp.bfloat16), "seq", scatter_dimension=0, tiled=True
        ).astype(jnp.float32),
        lax.psum_scatter(
            grad_list[3].astype(jnp.bfloat16), "seq", scatter_dimension=0, tiled=True
        ).astype(jnp.float32),
        lax.psum_scatter(
            grad_list[4].astype(jnp.bfloat16), "seq", scatter_dimension=0, tiled=True
        ).astype(jnp.float32),
        lax.psum_scatter(
            grad_list[5].astype(jnp.bfloat16), "seq", scatter_dimension=0, tiled=True
        ).astype(jnp.float32),
        lax.psum_scatter(
            grad_list[6].astype(jnp.bfloat16), "seq", scatter_dimension=0, tiled=True
        ).astype(jnp.float32),
        lax.psum_scatter(
            grad_list[7].astype(jnp.bfloat16), "seq", scatter_dimension=0, tiled=True
        ).astype(jnp.float32),
        lax.psum_scatter(
            grad_list[8].astype(jnp.bfloat16), "seq", scatter_dimension=0, tiled=True
        ).astype(jnp.float32),
        lax.psum_scatter(
            grad_list[9].astype(jnp.bfloat16), "seq", scatter_dimension=0, tiled=True
        ).astype(jnp.float32),
        lax.psum_scatter(
            grad_list[10].astype(jnp.bfloat16), "seq", scatter_dimension=0, tiled=True
        ).astype(jnp.float32),
        lax.psum_scatter(
            grad_list[11].astype(jnp.bfloat16), "seq", scatter_dimension=0, tiled=True
        ).astype(jnp.float32),
        lax.psum_scatter(
            grad_list[12].astype(jnp.bfloat16), "seq", scatter_dimension=0, tiled=True
        ).astype(jnp.float32),
        lax.psum_scatter(
            grad_list[13].astype(jnp.bfloat16), "seq", scatter_dimension=0, tiled=True
        ).astype(jnp.float32),
        lax.psum_scatter(
            grad_list[14].astype(jnp.bfloat16), "seq", scatter_dimension=0, tiled=True
        ).astype(jnp.float32),
        lax.psum_scatter(
            grad_list[15].astype(jnp.bfloat16), "seq", scatter_dimension=1, tiled=True
        ).astype(jnp.float32),
        lax.psum_scatter(
            grad_list[16].astype(jnp.bfloat16), "seq", scatter_dimension=1, tiled=True
        ).astype(jnp.float32),
    )
    shares = (
        lax.psum_scatter(within_group[0], "chain", scatter_dimension=0, tiled=True),
        lax.psum_scatter(within_group[1], "chain", scatter_dimension=0, tiled=True),
        lax.psum_scatter(within_group[2], "chain", scatter_dimension=0, tiled=True),
        lax.psum_scatter(within_group[3], "chain", scatter_dimension=0, tiled=True),
        lax.psum_scatter(within_group[4], "chain", scatter_dimension=0, tiled=True),
        lax.psum_scatter(within_group[5], "chain", scatter_dimension=0, tiled=True),
        lax.psum_scatter(within_group[6], "chain", scatter_dimension=0, tiled=True),
        lax.psum_scatter(within_group[7], "chain", scatter_dimension=0, tiled=True),
        lax.psum_scatter(within_group[8], "chain", scatter_dimension=0, tiled=True),
        lax.psum_scatter(within_group[9], "chain", scatter_dimension=0, tiled=True),
        lax.psum_scatter(within_group[10], "chain", scatter_dimension=0, tiled=True),
        lax.psum_scatter(within_group[11], "chain", scatter_dimension=0, tiled=True),
        lax.psum_scatter(within_group[12], "chain", scatter_dimension=0, tiled=True),
        lax.psum_scatter(within_group[13], "chain", scatter_dimension=0, tiled=True),
        lax.psum_scatter(within_group[14], "chain", scatter_dimension=0, tiled=True),
        lax.psum_scatter(within_group[15], "chain", scatter_dimension=1, tiled=True),
        lax.psum_scatter(within_group[16], "chain", scatter_dimension=1, tiled=True),
    )
    return (
        layer_out,
        input_grad,
        shares[0],
        shares[1],
        shares[2],
        shares[3],
        shares[4],
        shares[5],
        shares[6],
        shares[7],
        shares[8],
        shares[9],
        shares[10],
        shares[11],
        shares[12],
        shares[13],
        shares[14],
        shares[15],
        shares[16],
    )


def solution(mesh):
    placed = (
        P("chain", None, "seq", None),
        P("chain", None, "seq", None),
        P("chain", None),
        P("chain", None),
        P(("seq", "chain"), None),
        P(("seq", "chain"), None),
        P(("seq", "chain"), None),
        P(("seq", "chain"), None),
        P(("seq", "chain")),
        P(("seq", "chain")),
        P(("seq", "chain")),
        P(("seq", "chain")),
        P(("seq", "chain")),
        P(("seq", "chain"), None),
        P(("seq", "chain")),
        P(("seq", "chain"), None),
        P(("seq", "chain")),
        P(("seq", "chain")),
        P(("seq", "chain")),
        P(None, ("seq", "chain")),
        P(None, ("seq", "chain")),
    )
    return jax.shard_map(
        shards,
        mesh=mesh,
        in_specs=placed,
        out_specs=(
            P("chain", None, "seq", None),
            P("chain", None, "seq", None),
            P(("seq", "chain"), None),
            P(("seq", "chain"), None),
            P(("seq", "chain"), None),
            P(("seq", "chain"), None),
            P(("seq", "chain")),
            P(("seq", "chain")),
            P(("seq", "chain")),
            P(("seq", "chain")),
            P(("seq", "chain")),
            P(("seq", "chain"), None),
            P(("seq", "chain")),
            P(("seq", "chain"), None),
            P(("seq", "chain")),
            P(("seq", "chain")),
            P(("seq", "chain")),
            P(None, ("seq", "chain")),
            P(None, ("seq", "chain")),
        ),
        check_vma=False,
    )
```

profile of v0, /device:TPU:0, one launch (start us, length us, event | category | flops | bytes accessed | tf_op | source)
XLA Modules:
  0.0 1290.6 jit_solution(9188346175578972847)
XLA Ops:
  18.8 42.4 %all-reduce.34 = (bf16[768]{0:T(1024)(128)(2,1)S(1)}, bf16[768]{0:T(1024)(128)(2,1)S(1)}, bf16[768]{0:T(1024)(128)(2,1)S(1)}, bf16[768]{0:T(1024)(128)(2,1)S(1)}...) all-reduce(bf16[768]{0:T(1024)(128)(2,1)S(1)} %dynamic-update-slice, ...), channel_id=1, replica_groups=mesh['seq'=2,'chain'=16] {'seq','chain'}, use_global_device_ids=true, to_apply=%add | all-reduce | flops 9216 | bytes 36864
  61.2 41.0 %all-gather.1 = bf16[32,24,10]{1,2,0:T(8,128)(2,1)S(1)} all-gather(bf16[1,24,10]{1,2,0:T(8,128)(2,1)} %bitcast.199), channel_id=1, replica_groups=mesh['seq'=2,'chain'=16] {'seq','chain'}, dimensions={0}, use_global_device_ids=true | all-gather | bytes 15840 | tf_op jit(solution)/shard_map/all_gather | solution.py:112
  102.4 37.4 %all-gather = bf16[32,24,10]{1,2,0:T(8,128)(2,1)S(1)} all-gather(bf16[1,24,10]{1,2,0:T(8,128)(2,1)} %bitcast.200), channel_id=1, replica_groups=mesh['seq'=2,'chain'=16] {'seq','chain'}, dimensions={0}, use_global_device_ids=true | all-gather | bytes 15840 | tf_op jit(solution)/shard_map/all_gather | solution.py:111
  150.3 12.8 all-gather.2
  168.2 11.6 all-gather.17.cloned.1.call-done
  181.6 13.5 %all-gather.3 = bf16[2,276,768]{2,1,0:T(8,128)(2,1)S(1)} all-gather(bf16[1,276,768]{2,1,0:T(8,128)(2,1)S(1)} %fusion.32), channel_id=1, replica_groups=mesh['seq'=2,'chain'=16] {'seq'}, dimensions={0}, use_global_device_ids=true | all-gather | bytes 1271808 | tf_op jit(solution)/shard_map/all_gather | solution.py:166
  199.2 2.2 exponential_reduce_fusion.1
  202.5 2.3 convolution_convert_fusion.9
  204.9 30.7 %all-gather.19.cloned.1.call-done = bf16[768,768]{1,0:T(8,128)(2,1)} async-done(((bf16[24,768]{1,0:T(8,128)(2,1)}), bf16[768,768]{1,0:T(8,128)(2,1)}) %all-gather.19.cloned.1.call-update) | async-done | bytes 1179664 | tf_op jit(solution)/shard_map/all_gather | solution.py:99
  238.1 62.8 %all-gather.21.cloned.1.call-done = bf16[768,3072]{1,0:T(8,128)(2,1)} async-done(((bf16[24,3072]{1,0:T(8,128)(2,1)}), bf16[768,3072]{1,0:T(8,128)(2,1)}) %all-gather.21.cloned.1.call-update) | async-done | bytes 4718608 | tf_op jit(solution)/shard_map/all_gather | solution.py:105
  300.8 6.0 multiply_convert_fusion.3
  306.9 59.1 %all-gather.23.cloned.1.call-done = bf16[3072,768]{1,0:T(8,128)(2,1)} async-done(((bf16[96,768]{1,0:T(8,128)(2,1)}), bf16[3072,768]{1,0:T(8,128)(2,1)}) %all-gather.23.cloned.1.call-update) | async-done | bytes 4718608 | tf_op jit(solution)/shard_map/all_gather | solution.py:107
  366.0 4.6 fusion.108
  371.9 13.0 %all-gather.4 = bf16[2,276,768]{2,1,0:T(8,128)(2,1)} all-gather(bf16[1,276,768]{2,1,0:T(8,128)(2,1)S(1)} %fusion.34), channel_id=1, replica_groups=mesh['seq'=2,'chain'=16] {'seq'}, dimensions={0}, use_global_device_ids=true | all-gather | bytes 1271808 | tf_op jit(solution)/shard_map/all_gather | solution.py:167
  384.9 4.7 copy.73
  389.6 3.6 reshape.229
  393.2 2.3 fusion.31
  399.5 12.1 all-gather.5
  411.6 2.8 copy.75
  414.4 2.9 reshape.231
  417.4 2.8 fusion.1
  420.2 2.2 exponential_reduce_fusion
  424.6 2.3 convolution_convert_fusion.8
  428.2 2.2 multiply_convert_fusion.2
  435.4 3.2 convert_reduce_fusion.1
  438.6 2.4 multiply_reduce_fusion.5
  446.3 7.5 multiply_reduce_fusion.1
  453.9 3.3 convolution_convert_fusion.7
  457.2 2.4 multiply_convert_fusion.1
  465.0 4.5 convert_reduce_fusion.5
  472.0 50.9 %all-reduce.43.cloned.1.call-done = (bf16[552,768]{0,1:T(8,128)(2,1)}, bf16[552,768]{0,1:T(8,128)(2,1)}) async-done(((bf16[552,768]{0,1:T(8,128)(2,1)}, bf16[552,768]{0,1:T(8,128)(2,1)}), (bf16[552,768]{0,1:T(8,128)(2,1)}, bf16[552,768]{0,1:T(8,128)(2,1)})) %all-reduce.43.cloned.1.call-update) | async-done | bytes 1695760
  524.5 2.4 convert_reduce_fusion.3
  526.9 2.4 convolution_add_fusion.5
  531.0 7.7 psum.7
  541.3 5.0 convert_reduce_fusion
  546.4 2.4 multiply_reduce_fusion.4
  554.2 6.5 multiply_reduce_fusion
  560.8 3.3 convolution_convert_fusion.6
  564.1 2.4 multiply_convert_fusion
  570.6 9.0 concatenate.47
  579.6 3.9 convert_reduce_fusion.4
  584.4 2.4 convolution_convert_fusion.5
  587.1 3.5 convolution_convert_fusion.2
  590.6 41.7 %all-reduce.41.cloned.1.call-done = (bf16[552,768]{0,1:T(8,128)(2,1)}, bf16[552,768]{0,1:T(8,128)(2,1)}) async-done(((bf16[552,768]{0,1:T(8,128)(2,1)}, bf16[552,768]{0,1:T(8,128)(2,1)}), (bf16[552,768]{0,1:T(8,128)(2,1)}, bf16[552,768]{0,1:T(8,128)(2,1)})) %all-reduce.41.cloned.1.call-update) | async-done | bytes 1695760
  634.5 2.3 convolution_convert_fusion.4
  639.4 2.3 convolution_convert_fusion.3
  641.8 7.6 convolution_convert_fusion.1
  651.2 8.1 convolution_convert_fusion
  668.6 2.2 convert_element_type.403
  670.8 9.4 reduce-scatter.37.cloned.1.call-done
  682.5 21.8 %reduce-scatter.29.cloned.1.call-done = bf16[384,768]{1,0:T(8,128)(2,1)} async-done(((bf16[768,768]{1,0:T(8,128)(2,1)}), bf16[384,768]{1,0:T(8,128)(2,1)}) %reduce-scatter.29.cloned.1.call-update) | async-done | bytes 589840 | tf_op jit(solution)/shard_map/reduce_scatter | solution.py:341
  706.5 21.7 %reduce-scatter.33.cloned.1.call-done = bf16[384,768]{1,0:T(8,128)(2,1)} async-done(((bf16[768,768]{1,0:T(8,128)(2,1)}), bf16[384,768]{1,0:T(8,128)(2,1)}) %reduce-scatter.33.cloned.1.call-update) | async-done | bytes 589840 | tf_op jit(solution)/shard_map/reduce_scatter | solution.py:344
  730.7 59.9 %reduce-scatter.41.cloned.1.call-done = bf16[384,3072]{1,0:T(8,128)(2,1)} async-done(((bf16[768,3072]{1,0:T(8,128)(2,1)}), bf16[384,3072]{1,0:T(8,128)(2,1)}) %reduce-scatter.41.cloned.1.call-update) | async-done | bytes 2359312 | tf_op jit(solution)/shard_map/reduce_scatter | solution.py:365
  790.6 4.4 convert_element_type.428
  795.1 57.8 %reduce-scatter.45.cloned.1.call-done = bf16[1536,768]{1,0:T(8,128)(2,1)} async-done(((bf16[3072,768]{1,0:T(8,128)(2,1)}), bf16[1536,768]{1,0:T(8,128)(2,1)}) %reduce-scatter.45.cloned.1.call-update) | async-done | bytes 2359312 | tf_op jit(solution)/shard_map/reduce_scatter | solution.py:371
  852.9 4.2 convert_element_type.434
  863.5 7.1 all-reduce.35
  874.4 4.6 reduce-scatter.51.cloned.1.call-done
  880.0 62.4 %all-reduce.33 = (f32[384]{0:T(512)S(1)}, f32[384]{0:T(512)S(1)}, f32[384]{0:T(512)S(1)}, f32[384]{0:T(512)S(1)}, f32[384]{0:T(512)S(1)}, /*index=5*/f32[1536]{0...) all-reduce(f32[384]{0:T(512)S(1)} %dynamic-slice_convert_fusion.8, ...), channel_id=15, replica_groups=mesh['seq'=2,'chain'=16] {'chain'}, use_global_device_ids=true, to_apply=%region_38.39.clone | all-reduce | flops 12288 | bytes 82944
  949.1 53.4 %reduce-scatter.39.cloned.1.call-done = f32[24,768]{1,0:T(8,128)} async-done(((f32[384,768]{1,0:T(8,128)}), f32[24,768]{1,0:T(8,128)}) %reduce-scatter.39.cloned.1.call-update) | async-done | bytes 73744 | tf_op jit(solution)/shard_map/reduce_scatter | solution.py:394
  1002.5 61.3 %reduce-scatter.31.cloned.1.call-done = f32[24,768]{1,0:T(8,128)} async-done(((f32[384,768]{1,0:T(8,128)}), f32[24,768]{1,0:T(8,128)}) %reduce-scatter.31.cloned.1.call-update) | async-done | bytes 73744 | tf_op jit(solution)/shard_map/reduce_scatter | solution.py:392
  1063.8 61.1 %reduce-scatter.35.cloned.1.call-done = f32[24,768]{1,0:T(8,128)} async-done(((f32[384,768]{1,0:T(8,128)}), f32[24,768]{1,0:T(8,128)}) %reduce-scatter.35.cloned.1.call-update) | async-done | bytes 73744 | tf_op jit(solution)/shard_map/reduce_scatter | solution.py:393
  1124.9 79.1 %reduce-scatter.43.cloned.1.call-done = f32[24,3072]{1,0:T(8,128)} async-done(((f32[384,3072]{1,0:T(8,128)}), f32[24,3072]{1,0:T(8,128)}) %reduce-scatter.43.cloned.1.call-update) | async-done | bytes 294928 | tf_op jit(solution)/shard_map/reduce_scatter | solution.py:400
  1203.9 79.6 %reduce-scatter.47.cloned.1.call-done = f32[96,768]{1,0:T(8,128)} async-done(((f32[1536,768]{1,0:T(8,128)}), f32[96,768]{1,0:T(8,128)}) %reduce-scatter.47.cloned.1.call-update) | async-done | bytes 294928 | tf_op jit(solution)/shard_map/reduce_scatter | solution.py:402
  (436 shorter events, 114.7 us)
Async XLA Ops:
  7.2 140.0 %copy-start.27 = (bf16[1,2,256,768]{3,2,1,0:T(8,128)(2,1)S(1)}, bf16[1,2,256,768]{3,2,1,0:T(8,128)(2,1)}, u32[]{:S(2)}) copy-start(bf16[1,2,256,768]{3,2,1,0:T(8,128)(2,1)} %param.22) | copy-start | bytes 2359300
  7.2 141.3 %all-gather.13.cloned.1.call-start = ((), (), s32[]{:S(2)}) async-start(), calls=%async_computation.14 | async-start | bytes 1216512 | tf_op jit(solution)/shard_map/all_gather | solution.py:98
  7.9 158.2 %all-gather.15.cloned.1.call-start = ((), (), s32[]{:S(2)}) async-start(), calls=%async_computation.15 | async-start | bytes 1216512 | tf_op jit(solution)/shard_map/all_gather | solution.py:96
  8.7 171.2 %all-gather.17.cloned.1.call-start = ((), (), s32[]{:S(2)}) async-start(), calls=%async_computation.16 | async-start | bytes 1216512 | tf_op jit(solution)/shard_map/all_gather | solution.py:97
  9.4 226.1 %all-gather.19.cloned.1.call-start = ((), (), s32[]{:S(2)}) async-start(), calls=%async_computation.17 | async-start | bytes 1216512 | tf_op jit(solution)/shard_map/all_gather | solution.py:99
  10.0 290.8 %all-gather.21.cloned.1.call-start = ((), (), s32[]{:S(2)}) async-start(), calls=%async_computation.18 | async-start | bytes 4866048 | tf_op jit(solution)/shard_map/all_gather | solution.py:105
  10.6 355.4 %all-gather.23.cloned.1.call-start = ((), (), s32[]{:S(2)}) async-start(), calls=%async_computation.19 | async-start | bytes 4866048 | tf_op jit(solution)/shard_map/all_gather | solution.py:107
  11.2 511.8 %all-reduce.43.cloned.1.call-start = ((), (), s32[]{:S(2)}) async-start(), calls=%async_computation.35 | async-start | bytes 3932160
  140.0 230.9 %copy-start.69 = (f32[768]{0:T(1024)}, f32[768]{0:T(1024)S(1)}, u32[]{:S(2)}) copy-start(f32[768]{0:T(1024)S(1)} %convert_element_type.359) | copy-start | bytes 9220
  144.6 56.8 %copy-start.78 = (pred[552]{0:T(1024)(128)(4,1)}, pred[552]{0:T(1024)(128)(4,1)S(1)}, u32[]{:S(2)}) copy-start(pred[552]{0:T(1024)(128)(4,1)S(1)} %compare_select_fusion.1) | copy-start | bytes 1660
  145.3 277.2 %copy-start.80 = (pred[552]{0:T(1024)(128)(4,1)}, pred[552]{0:T(1024)(128)(4,1)S(1)}, u32[]{:S(2)}) copy-start(pred[552]{0:T(1024)(128)(4,1)S(1)} %compare_select_fusion) | copy-start | bytes 1660
  145.3 90.3 %copy-start.65 = (bf16[10,768]{1,0:T(8,128)(2,1)}, bf16[10,768]{1,0:T(8,128)(2,1)S(1)}, u32[]{:S(2)}) copy-start(bf16[10,768]{1,0:T(8,128)(2,1)S(1)} %bitcast_select_fusion) | copy-start | bytes 46084
  147.2 32.6 %copy-start.46 = (bf16[256,768]{1,0:T(8,128)(2,1)}, bf16[256,768]{1,0:T(8,128)(2,1)S(1)}, u32[]{:S(2)}) copy-start(bf16[256,768]{1,0:T(8,128)(2,1)S(1)} %get-tuple-element.91) | copy-start | bytes 1179652
  168.2 29.2 %copy-start.10 = (bf16[276,768]{0,1:T(8,128)(2,1)}, bf16[276,768]{0,1:T(8,128)(2,1)S(1)}, u32[]{:S(2)}) copy-start(bf16[276,768]{0,1:T(8,128)(2,1)S(1)} %copy.71) | copy-start | bytes 1271812
  202.5 33.0 %copy-start.47 = (bf16[256,768]{1,0:T(8,128)(2,1)S(1)}, bf16[256,768]{1,0:T(8,128)(2,1)}, u32[]{:S(2)}) copy-start(bf16[256,768]{1,0:T(8,128)(2,1)} %copy-done.46) | copy-start | bytes 1179652
  204.9 33.0 %copy-start.96 = (bf16[12,64,276]{2,1,0:T(8,128)(2,1)}, bf16[12,64,276]{2,1,0:T(8,128)(2,1)S(1)}, u32[]{:S(2)}) copy-start(bf16[12,64,276]{2,1,0:T(8,128)(2,1)S(1)} %convolution_convert_fusion.9) | copy-start | bytes 1271812
  237.5 128.5 %copy-start.4 = (f32[276,768]{1,0:T(8,128)}, f32[276,768]{1,0:T(8,128)S(1)}, u32[]{:S(2)}) copy-start(f32[276,768]{1,0:T(8,128)S(1)} %get-tuple-element.100) | copy-start | bytes 2543620
  237.5 128.5 %copy-start.74 = (f32[276]{0:T(512)}, f32[276]{0:T(512)S(1)}, u32[]{:S(2)}) copy-start(f32[276]{0:T(512)S(1)} %broadcast_multiply_fusion.11) | copy-start | bytes 3316
  237.8 128.2 %copy-start.76 = (f32[276]{0:T(512)}, f32[276]{0:T(512)S(1)}, u32[]{:S(2)}) copy-start(f32[276]{0:T(512)S(1)} %add_rsqrt_fusion.3) | copy-start | bytes 3316
  238.1 68.8 %copy-start.55 = (bf16[276,768]{1,0:T(8,128)(2,1)}, bf16[276,768]{1,0:T(8,128)(2,1)S(1)}, u32[]{:S(2)}) copy-start(bf16[276,768]{1,0:T(8,128)(2,1)S(1)} %fusion.61) | copy-start | bytes 1271812
  366.0 5.2 copy-start.19
  366.0 5.2 copy-start.49
  370.9 18.7 %copy-start.71 = (f32[276]{0:T(512)}, f32[276]{0:T(512)S(1)}, u32[]{:S(2)}) copy-start(f32[276]{0:T(512)S(1)} %add_rsqrt_fusion.2) | copy-start | bytes 3316
  371.2 55.8 %copy-start.67 = (bf16[10,768]{1,0:T(8,128)(2,1)}, bf16[10,768]{1,0:T(8,128)(2,1)S(1)}, u32[]{:S(2)}) copy-start(bf16[10,768]{1,0:T(8,128)(2,1)S(1)} %slice_select_fusion.4) | copy-start | bytes 46084
  371.9 21.3 %copy-start.13 = (bf16[768,768]{1,0:T(8,128)(2,1)S(1)}, bf16[768,768]{1,0:T(8,128)(2,1)}, u32[]{:S(2)}) copy-start(bf16[768,768]{1,0:T(8,128)(2,1)} %all-gather.15.cloned.1.call-done) | copy-start | bytes 3538948
  420.2 8.0 slice-start.6
  444.2 9.7 slice-start.3
  446.3 7.6 slice-start.4
  446.3 7.6 slice-start.5
  446.3 7.6 copy-start.29
  446.3 7.6 copy-start.64
  446.3 7.6 copy-start.81
  463.7 168.6 %all-reduce.41.cloned.1.call-start = ((), (), s32[]{:S(2)}) async-start(), calls=%async_computation.34 | async-start | bytes 3932160
  465.0 5.3 copy-start.14
  522.9 6.4 copy-start.20
  522.9 6.4 copy-start.26
  526.9 12.5 copy-start.8
  526.9 12.5 copy-start.72
  540.3 6.0 slice-start.8
  541.3 5.1 copy-start.77
  546.4 5.1 copy-start.18
  548.8 5.3 copy-start.23
  548.8 5.4 copy-start.62
  548.8 5.4 copy-start.79
  548.9 11.9 slice-start
  554.2 6.5 slice-start.1
  554.2 6.5 slice-start.2
  570.5 13.8 %copy-start.31 = (bf16[12,64,276]{2,1,0:T(8,128)(2,1)S(1)}, bf16[12,64,276]{2,1,0:T(8,128)(2,1)}, u32[]{:S(2)}) copy-start(bf16[12,64,276]{2,1,0:T(8,128)(2,1)} %copy-done.30) | copy-start | bytes 1271812
  570.5 98.0 %reduce-scatter.25.cloned.1.call-start = ((), (), s32[]{:S(2)}) async-start(), calls=%async_computation.20 | async-start | bytes 1769472 | tf_op jit(solution)/shard_map/reduce_scatter | solution.py:338
  586.8 47.7 %copy-start.36 = (bf16[276,768]{0,1:T(8,128)(2,1)S(1)}, bf16[276,768]{0,1:T(8,128)(2,1)}, u32[]{:S(2)}) copy-start(bf16[276,768]{0,1:T(8,128)(2,1)} %copy-done.35) | copy-start | bytes 1271812
  586.8 93.4 %reduce-scatter.37.cloned.1.call-start = ((), (), s32[]{:S(2)}) async-start(), calls=%async_computation.26 | async-start | bytes 1769472 | tf_op jit(solution)/shard_map/reduce_scatter | solution.py:347
  590.5 113.8 %reduce-scatter.29.cloned.1.call-start = ((), (), s32[]{:S(2)}) async-start(), calls=%async_computation.22 | async-start | bytes 1769472 | tf_op jit(solution)/shard_map/reduce_scatter | solution.py:341
  636.8 91.4 %reduce-scatter.33.cloned.1.call-start = ((), (), s32[]{:S(2)}) async-start(), calls=%async_computation.24 | async-start | bytes 1769472 | tf_op jit(solution)/shard_map/reduce_scatter | solution.py:344
  641.7 148.9 %reduce-scatter.41.cloned.1.call-start = ((), (), s32[]{:S(2)}) async-start(), calls=%async_computation.28 | async-start | bytes 7077888 | tf_op jit(solution)/shard_map/reduce_scatter | solution.py:365
  649.5 203.4 %reduce-scatter.45.cloned.1.call-start = ((), (), s32[]{:S(2)}) async-start(), calls=%async_computation.30 | async-start | bytes 7077888 | tf_op jit(solution)/shard_map/reduce_scatter | solution.py:371
  659.4 214.1 %reduce-scatter.49.cloned.1.call-start = ((), (), s32[]{:S(2)}) async-start(), calls=%async_computation.32 | async-start | bytes 294912
  667.6 211.5 %reduce-scatter.51.cloned.1.call-start = ((), (), s32[]{:S(2)}) async-start(), calls=%async_computation.33 | async-start | bytes 294912
  668.5 280.6 %reduce-scatter.27.cloned.1.call-start = ((), (), s32[]{:S(2)}) async-start(), calls=%async_computation.21 | async-start | bytes 1253376 | tf_op jit(solution)/shard_map/reduce_scatter | solution.py:391
  670.8 331.7 %reduce-scatter.39.cloned.1.call-start = ((), (), s32[]{:S(2)}) async-start(), calls=%async_computation.27 | async-start | bytes 1253376 | tf_op jit(solution)/shard_map/reduce_scatter | solution.py:394
  682.4 381.3 %reduce-scatter.31.cloned.1.call-start = ((), (), s32[]{:S(2)}) async-start(), calls=%async_computation.23 | async-start | bytes 1253376 | tf_op jit(solution)/shard_map/reduce_scatter | solution.py:392
  706.5 418.4 %reduce-scatter.35.cloned.1.call-start = ((), (), s32[]{:S(2)}) async-start(), calls=%async_computation.25 | async-start | bytes 1253376 | tf_op jit(solution)/shard_map/reduce_scatter | solution.py:393
  730.5 473.5 %reduce-scatter.43.cloned.1.call-start = ((), (), s32[]{:S(2)}) async-start(), calls=%async_computation.29 | async-start | bytes 5013504 | tf_op jit(solution)/shard_map/reduce_scatter | solution.py:400
  795.0 488.5 %reduce-scatter.47.cloned.1.call-start = ((), (), s32[]{:S(2)}) async-start(), calls=%async_computation.31 | async-start | bytes 5013504 | tf_op jit(solution)/shard_map/reduce_scatter | solution.py:402
  857.3 6.2 copy-start.85
  (75 other events, 239.1 us)
Sparse Core Ops, SparseCore 0:
  10.9 56.9 all-gather.12
  70.8 53.1 all-gather.14
  126.8 52.9 all-gather.16
  182.6 52.9 all-gather.18
  238.3 62.5 all-gather.20
  303.6 62.3 all-gather.22
  463.8 59.0 all-reduce.42
  570.6 61.5 all-reduce.40
  634.5 21.7 reduce-scatter.24
  658.5 21.7 reduce-scatter.36
  682.5 21.7 reduce-scatter.28
  706.5 21.7 reduce-scatter.32
  730.6 59.9 reduce-scatter.40
  792.9 59.9 reduce-scatter.44
  855.0 10.9 reduce-scatter.48
  868.0 10.9 reduce-scatter.50
  883.1 58.1 reduce-scatter.26
  945.3 57.1 reduce-scatter.38
  1006.7 57.0 reduce-scatter.30
  1067.8 57.0 reduce-scatter.34
  1129.3 74.5 reduce-scatter.42
  1208.9 74.6 reduce-scatter.46
where the time goes:
time: 1300 us; the launch traced here: 1290 us
  waiting for transfers between devices  770 us (59%)
  blocking collectives  250 us (19%)
  matrix products  120 us (9%)
  local copies, waits for them, and re-layouts  81.1 us (6%)
  other arithmetic  46.8 us (4%)
  between operations  21 us (2%)
    unnamed x3, blocking collectives  112 us
    unnamed x26, waiting for transfers between devices  101 us
    reduce_scatter x1, waiting for transfers between devices, shards(): lax.psum_scatter(within_group[11], 'chain', scatter_dimension=0, tiled=True)  79.6 us
    reduce_scatter x1, waiting for transfers between devices, shards(): lax.psum_scatter(within_group[9], 'chain', scatter_dimension=0, tiled=True)  79.1 us
    all_gather x1, waiting for transfers between devices, shards(): lax.all_gather(inner_weight, ('seq', 'chain'), axis=0, tiled=True)  62.8 us
    reduce_scatter x1, waiting for transfers between devices, shards(): lax.psum_scatter(within_group[1], 'chain', scatter_dimension=0, tiled=True)  61.3 us
    reduce_scatter x1, waiting for transfers between devices, shards(): lax.psum_scatter(within_group[2], 'chain', scatter_dimension=0, tiled=True)  61.1 us
    reduce_scatter x1, waiting for transfers between devices, shards(): lax.psum_scatter(grad_list[9].astype(jnp.bfloat16), 'seq', scatter_dimens...  59.9 us
  transfers between devices with their start and end apart: 22, of which 17 were waited for; matrix products, arithmetic and copies ran while one was open for 10% of the time, Pallas kernels for 0%

commit v1 on v0

v1 whole, which is shorter than its diff:
```python
import functools
import math

import jax
import jax.numpy as jnp
from jax import lax
from jax.experimental import pallas as pl
from jax.experimental.pallas import tpu as pltpu
from jax.sharding import PartitionSpec as P

HEADS = 12
MEM = 10
EPS = 1e-12
INV_ROOT_TWO = 1.0 / math.sqrt(2.0)
INV_ROOT_TWO_PI = 1.0 / math.sqrt(2.0 * math.pi)
NEG_FILL = -1000000000.0

MESH = pl.DeviceIdType.MESH


def place():
    seq = lax.axis_index("seq")
    chain = lax.axis_index("chain")
    return seq, chain // 4, lax.rem(chain // 2, 2), lax.rem(chain, 2)


def block_of(levels, seq, level, side, core):
    return seq * (4 * levels) + level * 4 + side * 2 + core


def device_of(seq, level, side, core):
    return (seq, level * 4 + side * 2 + core)


def greet(levels):
    seq, level, side, core = place()
    barrier = pltpu.get_barrier_semaphore()

    def tell(*target):
        pl.semaphore_signal(barrier, inc=1, device_id=device_of(*target), device_id_type=MESH)

    tell(seq, level, side, 1 - core)
    tell(seq, level, 1 - side, core)
    tell(1 - seq, level, side, core)

    @pl.when(level > 0)
    def _():
        tell(seq, level - 1, side, core)

    @pl.when(level < levels - 1)
    def _():
        tell(seq, level + 1, side, core)

    pl.semaphore_wait(
        barrier,
        3 + (level > 0).astype(jnp.int32) + (level < levels - 1).astype(jnp.int32),
    )


def gather_kernel(levels, parts, late, *refs):
    count = len(parts)
    arrays = 1 + max(p[0] for p in parts)
    shard_refs, whole_refs = refs[:arrays], refs[arrays : 2 * arrays]
    recv_sems, send_sems, own_sems = refs[2 * arrays :]
    seq, level, side, core = place()
    greet(levels)
    targets = {
        0: (seq, level, side, 1 - core),
        1: (seq, level, 1 - side, core),
        2: (1 - seq, level, side, core),
        3: (seq, level + 1, side, core),
        4: (seq, level - 1, side, core),
    }

    def block(step_seq, at, step_side, of_core):
        return block_of(
            levels, seq if step_seq == 0 else 1 - seq, at, side if step_side == 0 else 1 - side, of_core
        )

    def shard_view(part):
        array, row, rows, column, columns = parts[part]
        return shard_refs[array].at[pl.ds(row, rows), pl.ds(column, columns)]

    def whole_view(part, index):
        array, row, rows, column, columns = parts[part]
        return whole_refs[array].at[index, pl.ds(row, rows), pl.ds(column, columns)]

    def copy(part, index, kind, own=False):
        source = shard_view(part) if own else whole_view(part, index)
        return pltpu.make_async_remote_copy(
            src_ref=source,
            dst_ref=whole_view(part, index),
            send_sem=send_sems.at[part, index, kind],
            recv_sem=recv_sems.at[part, index],
            device_id=device_of(*targets[kind]),
            device_id_type=MESH,
        )

    def arrived(part, index):
        copy(part, index, 0).wait_recv()

    def over_column(part, index, own=False, plane=True):
        if plane:
            copy(part, index, 1, own).start()
            copy(part, index, 2, own).start()
        copy(part, index, 0, own).start()

    mine = block(0, level, 0, core)

    def up(part, index, own=False):
        @pl.when(level < levels - 1)
        def _():
            copy(part, index, 3, own).start()

    def down(part, index, own=False):
        @pl.when(level > 0)
        def _():
            copy(part, index, 4, own).start()

    def route(part):
        return part % 2

    for part in range(count):
        up(part, mine, True)
        down(part, mine, True)
        over_column(part, mine, True)
        pltpu.make_async_copy(shard_view(part), whole_view(part, mine), own_sems.at[part]).start()

    def from_plane(part, at):
        beside = block(0, at, 1, core)
        arrived(part, beside)
        if route(part) == 0:
            copy(part, beside, 2).start()
        copy(part, beside, 0).start()
        across = block(1, at, 0, core)
        arrived(part, across)
        if route(part) == 1:
            copy(part, across, 1).start()
        copy(part, across, 0).start()

    def from_corner(part, at):
        corner = block(1, at, 1, core)
        arrived(part, corner)
        copy(part, corner, 0).start()

    def guarded(at, body):
        pl.when(jnp.logical_and(at >= 0, at < levels))(body)

    for step in range(levels + 2):
        for part in range(count):
            if part in late:
                continue
            if 1 <= step < levels:
                for sign in (-1, 1):
                    at = level + sign * step

                    def column(part=part, at=at, sign=sign):
                        index = block(0, at, 0, core)
                        arrived(part, index)
                        (up if sign < 0 else down)(part, index)
                        over_column(part, index)

                    guarded(at, column)
            if 1 <= step < levels + 1:
                near = step - 1
                for sign in (-1, 1) if near else (1,):
                    at = level + sign * near
                    guarded(at, functools.partial(from_plane, part, at))
            if step >= 2:
                near = step - 2
                for sign in (-1, 1) if near else (1,):
                    at = level + sign * near
                    guarded(at, functools.partial(from_corner, part, at))
        if step == 1:
            for part in late:
                from_plane(part, level)
                for index in (block(0, level, 1, core), block(1, level, 0, core)):
                    up(part, index)
                    down(part, index)
        if step == 2:
            for part in late:
                from_corner(part, level)
                up(part, block(1, level, 1, core))
                down(part, block(1, level, 1, core))
        if step >= 2 and step - 1 < levels:
            far = step - 1
            for part in late:
                for sign in (-1, 1):
                    at = level + sign * far

                    def four(part=part, at=at, sign=sign):
                        for place_at in ((0, 0), (0, 1), (1, 0), (1, 1)):
                            index = block(place_at[0], at, place_at[1], core)
                            arrived(part, index)
                            (up if sign < 0 else down)(part, index)
                            copy(part, index, 0).start()

                    guarded(at, four)

    for part in range(count):
        def other(at, carry, part=part):
            for place_at in ((0, 0), (0, 1), (1, 0), (1, 1)):
                arrived(part, block(place_at[0], at, place_at[1], 1 - core))
            return carry

        lax.fori_loop(0, levels, other, 0)

    for part in range(count):
        pltpu.make_async_copy(shard_view(part), whole_view(part, mine), own_sems.at[part]).wait()

        def left(at, carry, part=part):
            for place_at in ((0, 0), (0, 1), (1, 0), (1, 1)):
                index = block(place_at[0], at, place_at[1], core)
                copy(part, index, 0).wait_send()
                in_plane = part in late
                if part in late:
                    here = at == level
                else:
                    here = True
                if place_at == (0, 0):
                    def sides():
                        copy(part, index, 1).wait_send()
                        copy(part, index, 2).wait_send()
                    if here is True: sides()
                    else: pl.when(here)(sides)
                if place_at == (0, 1) and route(part) == 0:
                    fn = lambda: copy(part, index, 2).wait_send()
                    if here is True: fn()
                    else: pl.when(here)(fn)
                if place_at == (1, 0) and route(part) == 1:
                    fn = lambda: copy(part, index, 1).wait_send()
                    if here is True: fn()
                    else: pl.when(here)(fn)
                if place_at == (0, 0) or part in late:
                    @pl.when(jnp.logical_and(at <= level, level < levels - 1))
                    def _():
                        copy(part, index, 3).wait_send()

                    @pl.when(jnp.logical_and(at >= level, level > 0))
                    def _():
                        copy(part, index, 4).wait_send()
            return carry

        lax.fori_loop(0, levels, left, 0)


def gather_all(levels, shards, parts, late):
    count, arrays = len(parts), len(shards)
    total = 8 * levels
    anywhere = pl.BlockSpec(memory_space=pl.ANY)
    return pl.pallas_call(
        functools.partial(gather_kernel, levels, parts, late),
        out_shape=[jax.ShapeDtypeStruct((total,) + s.shape, s.dtype) for s in shards],
        in_specs=[anywhere] * arrays,
        out_specs=[anywhere] * arrays,
        scratch_shapes=[
            pltpu.SemaphoreType.DMA((count, total)),
            pltpu.SemaphoreType.DMA((count, total, 5)),
            pltpu.SemaphoreType.DMA((count,)),
        ],
        compiler_params=pltpu.CompilerParams(collective_id=0, has_side_effects=True),
        name="gather_weights",
    )(*shards)


def scatter_kernel(levels, parts, *refs):
    count = len(parts)
    arrays = 1 + max(p[0] for p in parts)
    part_refs, out_refs = refs[:arrays], refs[arrays : 2 * arrays]
    at_ref = 2 * arrays
    core_refs, side_refs, seq_refs, below_refs, above_refs = (
        refs[at_ref + i * count : at_ref + (i + 1) * count] for i in range(5)
    )
    core_send, core_recv, side_send, side_recv, seq_send, seq_recv, up_send, up_recv, down_send, down_recv = refs[
        at_ref + 5 * count :
    ]
    seq, level, side, core = place()
    greet(levels)

    def block(rel, at, of_core):
        return block_of(
            levels, seq if rel < 2 else 1 - seq, at, side if rel % 2 == 0 else 1 - side, of_core
        )

    def view(part, index):
        array, row, rows, column, columns = parts[part]
        return part_refs[array].at[index, pl.ds(row, rows), pl.ds(column, columns)]

    def remote(source, target, send_sem, recv_sem, device):
        return pltpu.make_async_remote_copy(
            src_ref=source, dst_ref=target, send_sem=send_sem, recv_sem=recv_sem,
            device_id=device_of(*device), device_id_type=MESH,
        )

    def over_core(part, at, rel):
        slot = at * 4 + rel
        return remote(
            view(part, block(rel, at, 1 - core)), core_refs[part].at[slot],
            core_send.at[part, slot], core_recv.at[part, slot], (seq, level, side, 1 - core),
        )

    def over_side(part, at, rel, routed):
        slot = at * 2 + routed
        return remote(
            core_refs[part].at[at * 4 + rel], side_refs[part].at[slot],
            side_send.at[part, slot], side_recv.at[part, slot], (seq, level, 1 - side, core),
        )

    def over_seq(part, at, rel, routed):
        slot = at * 2 + routed
        return remote(
            core_refs[part].at[at * 4 + rel], seq_refs[part].at[slot],
            seq_send.at[part, slot], seq_recv.at[part, slot], (1 - seq, level, side, core),
        )

    def over_up(part, at):
        return remote(
            core_refs[part].at[at * 4], below_refs[part].at[at],
            up_send.at[part, at], up_recv.at[part, at], (seq, level + 1, side, core),
        )

    def over_down(part, at):
        return remote(
            core_refs[part].at[at * 4], above_refs[part].at[at],
            down_send.at[part, at], down_recv.at[part, at], (seq, level - 1, side, core),
        )

    def route(part):
        return part % 2

    def loop(body):
        def step(at, carry):
            body(at)
            return carry
        lax.fori_loop(0, levels, step, 0)

    def total(part, at, rel, *more):
        value = view(part, block(rel, at, core))[...].astype(jnp.float32)
        value = value + core_refs[part][at * 4 + rel].astype(jnp.float32)
        for ref in more:
            value = value + ref[...].astype(jnp.float32)
        return value

    def keep(part, at, rel, value):
        core_refs[part][at * 4 + rel] = value.astype(jnp.bfloat16)

    def start_core(part):
        for rel in (3, 1, 2, 0):
            loop(lambda at: over_core(part, at, rel).start())

    def stage_corner(part):
        def body(at):
            over_core(part, at, 3).wait_recv()
            keep(part, at, 3, total(part, at, 3))
            (over_side if route(part) == 0 else over_seq)(part, at, 3, 1).start()
        loop(body)

    def stage_plane(part):
        def body(at):
            over_core(part, at, 1).wait_recv()
            over_core(part, at, 2).wait_recv()
            if route(part) == 1:
                keep_first, first, keep_second = 2, 2, 1
                keep(part, at, 2, total(part, at, 2))
                over_seq(part, at, 2, 0).start()
                over_seq(part, at, 3, 1).wait_recv()
                keep(part, at, 1, total(part, at, 1, seq_refs[part].at[at * 2 + 1]))
                over_side(part, at, 1, 0).start()
            else:
                keep(part, at, 1, total(part, at, 1))
                over_side(part, at, 1, 0).start()
                over_side(part, at, 3, 1).wait_recv()
                keep(part, at, 2, total(part, at, 2, side_refs[part].at[at * 2 + 1]))
                over_seq(part, at, 2, 0).start()
        loop(body)

    def ready(part, at):
        over_core(part, at, 0).wait_recv()
        over_side(part, at, 1, 0).wait_recv()
        over_seq(part, at, 2, 0).wait_recv()

    def column_total(part, at, *more):
        return total(part, at, 0, side_refs[part].at[at * 2], seq_refs[part].at[at * 2], *more)

    def stage_line(part):
        def body(turn, carry):
            high = levels - 1 - turn

            @pl.when(level < high)
            def _():
                ready(part, high)

                @pl.when(level == 0)
                def _():
                    keep(part, high, 0, column_total(part, high))

                @pl.when(level > 0)
                def _():
                    over_up(part, high).wait_recv()
                    keep(part, high, 0, column_total(part, high, below_refs[part].at[high]))

                over_up(part, high).start()

            @pl.when(level > turn)
            def _():
                ready(part, turn)

                @pl.when(level == levels - 1)
                def _():
                    keep(part, turn, 0, column_total(part, turn))

                @pl.when(level < levels - 1)
                def _():
                    over_down(part, turn).wait_recv()
                    keep(part, turn, 0, column_total(part, turn, above_refs[part].at[turn]))

                over_down(part, turn).start()

            return carry

        lax.fori_loop(0, levels - 1, body, 0)

    def stage_last(part):
        array, row, rows, column, columns = parts[part]
        out = out_refs[array].at[pl.ds(row, rows), pl.ds(column, columns)]
        ready(part, level)
        out[...] = column_total(part, level)

        @pl.when(level > 0)
        def _():
            over_up(part, level).wait_recv()
            out[...] += below_refs[part][level].astype(jnp.float32)

        @pl.when(level < levels - 1)
        def _():
            over_down(part, level).wait_recv()
            out[...] += above_refs[part][level].astype(jnp.float32)

    stages = (start_core, stage_corner, stage_plane, stage_line, stage_last)
    for turn in range(count + len(stages) - 1):
        for depth in range(len(stages)):
            if 0 <= turn - depth < count:
                stages[depth](turn - depth)

    for part in range(count):
        def left(at, part=part):
            for rel in range(4):
                over_core(part, at, rel).wait_send()
            over_side(part, at, 1, 0).wait_send()
            over_seq(part, at, 2, 0).wait_send()
            (over_side if route(part) == 0 else over_seq)(part, at, 3, 1).wait_send()

            @pl.when(at > level)
            def _():
                over_up(part, at).wait_send()

            @pl.when(at < level)
            def _():
                over_down(part, at).wait_send()
        loop(left)


def scatter_all(levels, grads, parts):
    count, arrays = len(parts), len(grads)
    sizes = [(p[2], p[4]) for p in parts]
    inside = pl.BlockSpec(memory_space=pltpu.VMEM)
    scratch = []
    for blocks in (4 * levels, 2 * levels, 2 * levels, levels, levels):
        scratch += [pltpu.VMEM((blocks,) + size, jnp.bfloat16) for size in sizes]
    for blocks in (4 * levels, 2 * levels, 2 * levels, levels, levels):
        scratch += [pltpu.SemaphoreType.DMA((count, blocks))] * 2
    return pl.pallas_call(
        functools.partial(scatter_kernel, levels, parts),
        out_shape=[jax.ShapeDtypeStruct(g.shape[1:], jnp.float32) for g in grads],
        in_specs=[inside] * arrays,
        out_specs=[inside] * arrays,
        scratch_shapes=scratch,
        compiler_params=pltpu.CompilerParams(
            collective_id=1, has_side_effects=True, vmem_limit_bytes=60 * 2**20
        ),
        name="scatter_grads",
    )(*grads)


def fori(count, body):
    def step(index, carry):
        body(index)
        return carry

    lax.fori_loop(0, count, step, 0)


def span(index, size):
    return pl.ds(pl.multiple_of(index * size, size), size)


def dot_nn(former, latter):
    return jnp.dot(former, latter, preferred_element_type=jnp.float32)


def dot_nt(former, latter):
    return lax.dot_general(former, latter, (((1,), (1,)), ((), ())), preferred_element_type=jnp.float32)


def dot_tn(former, latter):
    return lax.dot_general(former, latter, (((0,), (0,)), ((), ())), preferred_element_type=jnp.float32)


def fold(rows):
    return jnp.sum(rows.reshape(rows.shape[0] // 8, 8, rows.shape[1]), axis=0)


TILE = 256
CHUNK = 48
MEMORY = 32
LANES = 128


def middle_kernel(
    start_ref,
    mask_ref,
    token_ref,
    other_ref,
    cot_ref,
    vec_ref,
    inner_bias_ref,
    query_hbm,
    key_hbm,
    value_hbm,
    output_hbm,
    inner_hbm,
    outer_hbm,
    layer_ref,
    own_ref,
    pair_ref,
    small_ref,
    inner_bias_grad_ref,
    query_grad_hbm,
    key_grad_hbm,
    value_grad_hbm,
    output_grad_hbm,
    inner_grad_hbm,
    outer_grad_hbm,
    wq,
    wk,
    wv,
    wo,
    wi,
    w2,
    hid,
    query,
    key,
    value,
    probs,
    mixed,
    normed_one,
    normed_two,
    inverse_one,
    inverse_two,
    first_b,
    slope,
    active,
    grad_two_b,
    grad_one_b,
    grad_mixed,
    grad_query,
    grad_key,
    grad_value,
    work,
    memory,
    send_rows,
    recv_rows,
    stage,
    load_sems,
    stage_sems,
    pair_sems,
):
    slots, half, width = token_ref.shape
    rows = half + MEMORY
    keys = rows + half
    hidden_width = wi.shape[1]
    pairs = width // LANES
    scale = 1.0 / math.sqrt(width // HEADS)
    seq = lax.axis_index("seq")
    chain = lax.axis_index("chain")
    is_owner = seq == 0
    barrier = pltpu.get_barrier_semaphore()
    pl.semaphore_signal(barrier, inc=1, device_id=(1 - seq, chain), device_id_type=MESH)
    loads = [
        pltpu.make_async_copy(source, target, load_sems.at[i])
        for i, (source, target) in enumerate(
            (
                (query_hbm, wq),
                (key_hbm, wk),
                (value_hbm, wv),
                (output_hbm, wo),
                (inner_hbm, wi),
                (outer_hbm, w2),
            )
        )
    ]
    for load in loads:
        load.start()
    line = 2 * MEM

    def vec(at):
        return vec_ref[line + at : line + at + 1, :]

    def vec_tile(at, index):
        return vec_ref[line + at : line + at + 1, span(index, TILE)]

    lane = lax.broadcasted_iota(jnp.int32, (1, LANES), 1)
    low_half = lane < LANES // 2
    mem_row = lax.broadcasted_iota(jnp.int32, (MEMORY, 1), 0)
    tiles = width // TILE

    def half_of(values, which, factor):
        keep = low_half if which == 0 else jnp.logical_not(low_half)
        return values * jnp.where(keep, factor, 0.0).astype(values.dtype)

    def forward(slot):
        query_rows = pl.ds(half, rows)
        hid[slot, 0:half] = other_ref[slot]
        hid[slot, half : 2 * half] = token_ref[slot]
        initial = jnp.where(mem_row < line, vec_ref[0:MEMORY, :], 0.0)
        if slot > 0:
            second = work[half:rows].astype(jnp.bfloat16).astype(jnp.float32)
            carried = pltpu.roll(second, MEMORY - MEM, 0)
        else:
            carried = jnp.zeros_like(initial)
        restart = start_ref[slot] == 1
        initial = jnp.where(jnp.logical_or(mem_row >= MEM, restart), initial, carried)
        hid[slot, 2 * half : keys] = initial.astype(jnp.bfloat16)
        if slot == 0:
            loads[0].wait()

        def query_tile(j):
            query[slot, :, span(j, TILE)] = (
                dot_nn(hid[slot, query_rows], wq[:, span(j, TILE)]) + vec_tile(0, j)
            ).astype(jnp.bfloat16)

        fori(tiles, query_tile)
        if slot == 0:
            loads[1].wait()

        def key_tile(j):
            key[slot, :, span(j, TILE)] = dot_nn(hid[slot], wk[:, span(j, TILE)]).astype(jnp.bfloat16)

        fori(tiles, key_tile)
        if slot == 0:
            loads[2].wait()

        def value_tile(j):
            value[slot, :, span(j, TILE)] = (dot_nn(hid[slot], wv[:, span(j, TILE)]) + vec_tile(1, j)).astype(
                jnp.bfloat16
            )

        fori(tiles, value_tile)
        valid = mask_ref[slot]

        def attend(p):
            here = span(p, LANES)
            query_pair = query[slot, :, here]
            key_pair = key[slot, :, here]
            value_pair = value[slot, :, here]
            sides = []
            for which in range(2):
                scores = dot_nt(half_of(query_pair, which, scale), key_pair) + valid
                top = jnp.max(scores, axis=1, keepdims=True)
                raised = jnp.exp(scores - top)
                total = jnp.sum(raised, axis=1, keepdims=True)
                share = (raised * (1.0 / total)).astype(jnp.bfloat16)
                probs[slot, 2 * p + which] = share
                sides.append(dot_nn(share, value_pair))
            mixed[slot, :, here] = jnp.where(low_half, sides[0], sides[1]).astype(jnp.bfloat16)

        fori(pairs, attend)
        if slot == 0:
            loads[3].wait()

        def branch_tile(j):
            here = span(j, TILE)
            work[:, here] = (
                dot_nn(mixed[slot], wo[:, here]) + vec_tile(2, j) + hid[slot, query_rows, here].astype(jnp.float32)
            )

        fori(tiles, branch_tile)

        def norm_chunk(normed, inverse, gain_at, shift_at):
            def body(r):
                here = span(r, CHUNK)
                z = work[here, :]
                centred = z - jnp.mean(z, axis=1, keepdims=True)
                inv = lax.rsqrt(jnp.mean(centred * centred, axis=1, keepdims=True) + EPS)
                unit = centred * inv
                normed[slot, here] = unit.astype(jnp.bfloat16)
                inverse[slot, here] = inv
                out = unit * vec(gain_at) + vec(shift_at)
                work[here, :] = out
                if normed is normed_one:
                    first_b[slot, here] = out.astype(jnp.bfloat16)

            return body

        fori(rows // CHUNK, norm_chunk(normed_one, inverse_one, 3, 4))
        if slot == 0:
            loads[4].wait()

        def inner_tile(j):
            here = span(j, TILE)
            u = dot_nn(first_b[slot], wi[:, here]) + inner_bias_ref[:, here]
            cumulative = 0.5 * (1.0 + lax.erf(u * INV_ROOT_TWO))
            density = jnp.exp(-0.5 * u * u) * INV_ROOT_TWO_PI
            active[slot, :, here] = (u * cumulative).astype(jnp.bfloat16)
            slope[slot, :, here] = (cumulative + u * density).astype(jnp.bfloat16)

        fori(hidden_width // TILE, inner_tile)
        if slot == 0:
            loads[5].wait()

        def outer_tile(j):
            here = span(j, TILE)
            work[:, here] += dot_nn(active[slot], w2[:, here]) + vec_tile(5, j)

        fori(tiles, outer_tile)
        fori(rows // CHUNK, norm_chunk(normed_two, inverse_two, 6, 7))
        layer_ref[slot] = work[0:half].astype(jnp.bfloat16)

    def add_small(at, folded):
        small_ref[line + at : line + at + 1, :] += jnp.sum(folded, axis=0, keepdims=True)

    def backward(slot):
        work[0:half] = cot_ref[slot].astype(jnp.float32)
        work[half:rows] = memory[...]

        def norm_back_pass(normed, inverse, gain_at, shift_at, bias_at, rounded):
            zero = jnp.zeros((8, width), jnp.float32)

            def body(r, sums):
                here = span(r, CHUNK)
                grad = work[here, :]
                unit = normed[slot, here].astype(jnp.float32)
                gain_sum = sums[0] + fold(grad * unit)
                shift_sum = sums[1] + fold(grad)
                scaled = grad * vec(gain_at)
                dz = inverse[slot, here] * (
                    scaled
                    - jnp.mean(scaled, axis=1, keepdims=True)
                    - unit * jnp.mean(scaled * unit, axis=1, keepdims=True)
                )
                work[here, :] = dz
                dz_b = dz.astype(jnp.bfloat16)
                rounded[slot, here] = dz_b
                return (gain_sum, shift_sum, sums[2] + fold(dz_b.astype(jnp.float32)))

            sums = lax.fori_loop(0, rows // CHUNK, body, (zero, zero, zero))
            add_small(gain_at, sums[0])
            add_small(shift_at, sums[1])
            add_small(bias_at, sums[2])

        norm_back_pass(normed_two, inverse_two, 6, 7, 5, grad_two_b)

        def inner_tile(j):
            here = span(j, TILE)
            grad = (dot_nt(grad_two_b[slot], w2[here, :]) * slope[slot, :, here].astype(jnp.float32)).astype(
                jnp.bfloat16
            )
            slope[slot, :, here] = grad
            inner_bias_grad_ref[:, here] += jnp.sum(grad.astype(jnp.float32), axis=0, keepdims=True)

        fori(hidden_width // TILE, inner_tile)

        def first_tile(j):
            here = span(j, TILE)
            work[:, here] += dot_nt(slope[slot], wi[here, :])

        fori(tiles, first_tile)
        norm_back_pass(normed_one, inverse_one, 3, 4, 2, grad_one_b)

        def mixed_tile(j):
            here = span(j, TILE)
            grad_mixed[:, here] = dot_nt(grad_one_b[slot], wo[here, :]).astype(jnp.bfloat16)

        fori(tiles, mixed_tile)

        def attend(p):
            here = span(p, LANES)
            query_pair = query[slot, :, here]
            key_pair = key[slot, :, here]
            value_pair = value[slot, :, here]
            mixed_pair = grad_mixed[:, here]
            dq, dk, dv = [], [], []
            for which in range(2):
                share = probs[slot, 2 * p + which]
                grad = dot_nt(half_of(mixed_pair, which, 1.0), value_pair)
                soft = share.astype(jnp.float32)
                delta = jnp.sum(grad * soft, axis=1, keepdims=True)
                grad_b = (soft * (grad - delta)).astype(jnp.bfloat16)
                dq.append(dot_nn(grad_b, key_pair))
                dk.append(dot_tn(grad_b, query_pair))
                dv.append(dot_tn(share, mixed_pair))
            dq_b = (jnp.where(low_half, dq[0], dq[1]) * scale).astype(jnp.bfloat16)
            dv_b = jnp.where(low_half, dv[0], dv[1]).astype(jnp.bfloat16)
            grad_query[slot, :, here] = dq_b
            grad_key[slot, :, here] = (jnp.where(low_half, dk[0], dk[1]) * scale).astype(jnp.bfloat16)
            grad_value[slot, :, here] = dv_b
            small_ref[line : line + 1, here] += jnp.sum(dq_b.astype(jnp.float32), axis=0, keepdims=True)
            small_ref[line + 1 : line + 2, here] += jnp.sum(dv_b.astype(jnp.float32), axis=0, keepdims=True)

        fori(pairs, attend)

        def input_tile(j):
            here = span(j, TILE)
            both = dot_nt(grad_key[slot], wk[here, :]) + dot_nt(grad_value[slot], wv[here, :])
            pair_ref[slot, :, here] = both[0:half].astype(jnp.bfloat16)
            mine = both[half:keys] + dot_nt(grad_query[slot], wq[here, :]) + work[:, here]
            own_ref[slot, :, here] = mine[0:half]
            memory[:, here] = mine[half:rows]

        fori(tiles, input_tile)
        restart = start_ref[slot] == 1
        grads = memory[...]
        counted = jnp.logical_or(
            jnp.logical_and(mem_row < MEM, restart), jnp.logical_and(mem_row >= MEM, mem_row < line)
        )
        small_ref[0:MEMORY, :] += jnp.where(counted, grads, 0.0)
        if slot > 0:
            passed = jnp.where(jnp.logical_and(mem_row < MEM, jnp.logical_not(restart)), grads, 0.0)
            send_rows[...] = passed
            pl.semaphore_wait(barrier, 1)
            swap = pltpu.make_async_remote_copy(
                src_ref=send_rows,
                dst_ref=recv_rows,
                send_sem=pair_sems.at[0],
                recv_sem=pair_sems.at[1],
                device_id=(1 - seq, chain),
                device_id_type=MESH,
            )
            swap.start()
            swap.wait()
            summed = pltpu.roll(passed + recv_rows[...], MEM, 0)
            memory[...] = jnp.where(is_owner, summed, 0.0)

    small_ref[...] = jnp.zeros_like(small_ref)
    inner_bias_grad_ref[...] = jnp.zeros_like(inner_bias_grad_ref)
    for slot in range(slots):
        forward(slot)
    memory[...] = jnp.zeros_like(memory)
    for slot in reversed(range(slots)):
        backward(slot)

    def emit(count, compute, target):
        def copy(j):
            buffer = lax.rem(j, 2)
            return pltpu.make_async_copy(stage.at[buffer], target(j), stage_sems.at[buffer])

        def body(j):
            @pl.when(j >= 2)
            def _():
                copy(j - 2).wait()

            stage[lax.rem(j, 2)] = compute(j).astype(jnp.bfloat16)
            copy(j).start()

        fori(count, body)
        copy(count - 2).wait()
        copy(count - 1).wait()

    def product(former, latter):
        total = None
        for slot in range(slots):
            term = dot_tn(former(slot), latter(slot))
            total = term if total is None else total + term
        return total

    emit(
        tiles,
        lambda j: product(lambda s: hid[s, half:keys, span(j, TILE)], lambda s: grad_query[s]),
        lambda j: query_grad_hbm.at[span(j, TILE)],
    )
    emit(
        tiles,
        lambda j: product(lambda s: hid[s, :, span(j, TILE)], lambda s: grad_key[s]),
        lambda j: key_grad_hbm.at[span(j, TILE)],
    )
    emit(
        tiles,
        lambda j: product(lambda s: hid[s, :, span(j, TILE)], lambda s: grad_value[s]),
        lambda j: value_grad_hbm.at[span(j, TILE)],
    )
    emit(
        tiles,
        lambda j: product(lambda s: mixed[s, :, span(j, TILE)], lambda s: grad_one_b[s]),
        lambda j: output_grad_hbm.at[span(j, TILE)],
    )
    emit(
        hidden_width // TILE,
        lambda j: product(
            lambda s: first_b[s, :, span(lax.rem(j, tiles), TILE)], lambda s: slope[s, :, span(j // tiles, width)]
        ),
        lambda j: inner_grad_hbm.at[span(lax.rem(j, tiles), TILE), span(j // tiles, width)],
    )
    emit(
        hidden_width // TILE,
        lambda j: product(lambda s: active[s, :, span(j, TILE)], lambda s: grad_two_b[s]),
        lambda j: outer_grad_hbm.at[span(j, TILE)],
    )


def middle(start, mask, tokens, others, cotangent, vectors, inner_bias, weights):
    slots, half, width = tokens.shape
    rows, keys = half + MEMORY, 2 * half + MEMORY
    hidden_width = inner_bias.shape[1]
    bf16, f32 = jnp.bfloat16, jnp.float32
    inside = pl.BlockSpec(memory_space=pltpu.VMEM)
    anywhere = pl.BlockSpec(memory_space=pl.ANY)
    shape = jax.ShapeDtypeStruct
    dma = pltpu.SemaphoreType.DMA
    return pl.pallas_call(
        middle_kernel,
        out_shape=[
            shape((slots, half, width), bf16),
            shape((slots, half, width), f32),
            shape((slots, half, width), bf16),
            shape((MEMORY, width), f32),
            shape((1, hidden_width), f32),
        ]
        + [shape(w.shape, bf16) for w in weights],
        in_specs=[pl.BlockSpec(memory_space=pltpu.SMEM)] + [inside] * 6 + [anywhere] * 6,
        out_specs=[inside] * 5 + [anywhere] * 6,
        scratch_shapes=[pltpu.VMEM(w.shape, bf16) for w in weights]
        + [
            pltpu.VMEM((slots, keys, width), bf16),
            pltpu.VMEM((slots, rows, width), bf16),
            pltpu.VMEM((slots, keys, width), bf16),
            pltpu.VMEM((slots, keys, width), bf16),
            pltpu.VMEM((slots, HEADS, rows, keys), bf16),
            pltpu.VMEM((slots, rows, width), bf16),
            pltpu.VMEM((slots, rows, width), bf16),
            pltpu.VMEM((slots, rows, width), bf16),
            pltpu.VMEM((slots, rows, 1), f32),
            pltpu.VMEM((slots, rows, 1), f32),
            pltpu.VMEM((slots, rows, width), bf16),
            pltpu.VMEM((slots, rows, hidden_width), bf16),
            pltpu.VMEM((slots, rows, hidden_width), bf16),
            pltpu.VMEM((slots, rows, width), bf16),
            pltpu.VMEM((slots, rows, width), bf16),
            pltpu.VMEM((rows, width), bf16),
            pltpu.VMEM((slots, rows, width), bf16),
            pltpu.VMEM((slots, keys, width), bf16),
            pltpu.VMEM((slots, keys, width), bf16),
            pltpu.VMEM((rows, width), f32),
            pltpu.VMEM((MEMORY, width), f32),
            pltpu.VMEM((MEMORY, width), f32),
            pltpu.VMEM((MEMORY, width), f32),
            pltpu.VMEM((2, TILE, width), bf16),
            dma((6,)),
            dma((2,)),
            dma((2,)),
        ],
        compiler_params=pltpu.CompilerParams(
            collective_id=2, has_side_effects=True, vmem_limit_bytes=62 * 2**20
        ),
        cost_estimate=pl.CostEstimate(flops=31 * 10**9, bytes_accessed=40 * 10**6, transcendentals=10**7),
        name="layer",
    )(start, mask, tokens, others, cotangent, vectors, inner_bias, *weights)


def small_block(vectors, inner_bias, read_init, write_init):
    width = vectors[0].shape[0]
    inner_width = inner_bias.shape[0]
    rows = jnp.concatenate([read_init, write_init] + [v[None] for v in vectors], axis=0)
    rows = jnp.pad(rows, ((0, 4), (0, 128 - width)))
    return rows + jnp.pad(inner_bias[None], ((28, 3), (0, 128 - inner_width)))


def shards(
    tokens,
    cotangent,
    chain_start,
    seg_len,
    query_weight,
    key_weight,
    value_weight,
    output_weight,
    query_bias,
    value_bias,
    output_bias,
    first_gain,
    first_shift,
    inner_weight,
    inner_bias,
    outer_weight,
    outer_bias,
    second_gain,
    second_shift,
    read_init,
    write_init,
):
    slot_count = tokens.shape[1]
    half_rows = tokens.shape[2]
    model_width = tokens.shape[3]
    blocks = lax.axis_size("seq") * lax.axis_size("chain")
    levels = lax.axis_size("chain") // 4
    width = model_width // blocks
    inner_columns = inner_weight.shape[1]
    inner_width = inner_bias.shape[0]
    kernels = width % 8 == 0
    small = small_block(
        (query_bias, value_bias, output_bias, first_gain, first_shift, outer_bias, second_gain, second_shift),
        inner_bias,
        read_init,
        write_init,
    )
    shard_list = [query_weight, key_weight, value_weight, output_weight, inner_weight, outer_weight, small]
    parts = [(i, 0, width, 0, model_width) for i in range(4)]
    parts += [(4, 0, width, 0, inner_columns // 2), (4, 0, width, inner_columns // 2, inner_columns // 2)]
    parts += [(5, 0, inner_width // 2, 0, model_width), (5, inner_width // 2, inner_width // 2, 0, model_width)]
    parts += [(6, 0, 32, 0, 128)]
    pair = [(0, 1), (1, 0)]
    others = lax.ppermute(tokens[0], "seq", pair)
    if kernels:
        whole = gather_all(levels, shard_list, parts, (7,))
    else:
        whole = [lax.all_gather(w, ("seq", "chain"), axis=0) for w in shard_list]
    whole_query, whole_key, whole_value, whole_output, whole_inner, whole_outer = (
        w.reshape(-1, w.shape[-1]) for w in whole[:6]
    )
    small_all = whole[6]
    vectors = small_all[:, :, :width].transpose(1, 0, 2).reshape(32, model_width).astype(jnp.float32)
    bias_inner = small_all[:, 28, :inner_width].reshape(1, -1).astype(jnp.float32)
    my_index = lax.axis_index("seq")
    place_in = jnp.arange(half_rows)
    position = jnp.concatenate(
        [
            (1 - my_index) * half_rows + place_in,
            my_index * half_rows + place_in,
            jnp.where(jnp.arange(MEMORY) < 2 * MEM, -1, 1 << 30),
        ]
    )
    mask = jnp.where(position[None, :] < seg_len[0][:, None], 0.0, NEG_FILL)[:, None, :]
    results = middle(
        chain_start[0],
        mask,
        tokens[0],
        others,
        cotangent[0],
        vectors,
        bias_inner,
        (whole_query, whole_key, whole_value, whole_output, whole_inner, whole_outer),
    )
    layer_out = results[0][None]
    received = lax.ppermute(results[2], "seq", pair)
    input_grad = (results[1] + received.astype(jnp.float32)).astype(jnp.bfloat16)[None]
    small_grads = jnp.pad(
        results[3].reshape(32, blocks, width).transpose(1, 0, 2), ((0, 0), (0, 0), (0, 128 - width))
    )
    inner_rows = jnp.pad(results[4].reshape(blocks, 1, inner_width), ((0, 0), (28, 3), (0, 128 - inner_width)))
    small_grads = jnp.where(jnp.arange(32)[None, :, None] == 28, inner_rows, small_grads).astype(jnp.bfloat16)
    weight_grads = [g.reshape((blocks,) + s.shape) for g, s in zip(results[5:], shard_list)]
    partial_grads = weight_grads + [small_grads]
    if kernels:
        sums = scatter_all(levels, partial_grads, parts)
    else:
        sums = [
            lax.psum_scatter(
                lax.psum_scatter(
                    g.reshape((-1,) + g.shape[2:]), "seq", scatter_dimension=0, tiled=True
                ).astype(jnp.float32),
                "chain", scatter_dimension=0, tiled=True,
            )
            for g in partial_grads
        ]
    small_sum = sums[6].reshape(32, 128)
    vector = [small_sum[20 + i, :width] for i in range(8)]
    return (
        layer_out,
        input_grad,
        sums[0],
        sums[1],
        sums[2],
        sums[3],
        vector[0],
        vector[1],
        vector[2],
        vector[3],
        vector[4],
        sums[4],
        small_sum[28, :inner_width],
        sums[5],
        vector[5],
        vector[6],
        vector[7],
        small_sum[:MEM, :width],
        small_sum[MEM : 2 * MEM, :width],
    )


def solution(mesh):
    placed = (
        P("chain", None, "seq", None),
        P("chain", None, "seq", None),
        P("chain", None),
        P("chain", None),
        P(("seq", "chain"), None),
        P(("seq", "chain"), None),
        P(("seq", "chain"), None),
        P(("seq", "chain"), None),
        P(("seq", "chain")),
        P(("seq", "chain")),
        P(("seq", "chain")),
        P(("seq", "chain")),
        P(("seq", "chain")),
        P(("seq", "chain"), None),
        P(("seq", "chain")),
        P(("seq", "chain"), None),
        P(("seq", "chain")),
        P(("seq", "chain")),
        P(("seq", "chain")),
        P(None, ("seq", "chain")),
        P(None, ("seq", "chain")),
    )
    return jax.shard_map(
        shards,
        mesh=mesh,
        in_specs=placed,
        out_specs=(
            P("chain", None, "seq", None),
            P("chain", None, "seq", None),
            P(("seq", "chain"), None),
            P(("seq", "chain"), None),
            P(("seq", "chain"), None),
            P(("seq", "chain"), None),
            P(("seq", "chain")),
            P(("seq", "chain")),
            P(("seq", "chain")),
            P(("seq", "chain")),
            P(("seq", "chain")),
            P(("seq", "chain"), None),
            P(("seq", "chain")),
            P(("seq", "chain"), None),
            P(("seq", "chain")),
            P(("seq", "chain")),
            P(("seq", "chain")),
            P(None, ("seq", "chain")),
            P(None, ("seq", "chain")),
        ),
        check_vma=False,
    )
```

time: 1300 us -> 356 us (0.27)
  waiting for transfers between devices: 770 us -> 0.01 us
  Pallas kernels: 0 us -> 327 us
  blocking collectives: 250 us -> 0 us
  matrix products: 120 us -> 0 us
  local copies, waits for them, and re-layouts: 81.1 us -> 16.7 us
  other arithmetic: 46.8 us -> 7.09 us
  between operations: 21 us -> 0.79 us
    reduce_scatter x12 -> x0, waiting for transfers between devices: 505 us -> none  [the longest x1 79.6 us: shards(): lax.psum_scatter(within_group[11], 'chain', scatter_dimension=0, tiled=True)]
    pallas_call x0 -> x3, Pallas kernels: none -> 327 us  [the longest x1 122 us: middle(): pl.pallas_call(middle_kernel, out_shape=[shape((slots, half, width), bf16...]
    all_gather x6 -> x0, waiting for transfers between devices: 164 us -> none  [the longest x1 62.8 us: shards(): lax.all_gather(inner_weight, ('seq', 'chain'), axis=0, tiled=True)]
    all_gather x6 -> x0, blocking collectives: 130 us -> none  [the longest x1 41 us: shards(): lax.all_gather(write_init, ('seq', 'chain'), axis=1, tiled=True)]
    dot_general x42 -> x0, matrix products: 120 us -> none  [the longest x12 27.3 us: matmul(): return jnp.dot(former, latter, preferred_element_type=jnp.float32)]
    unnamed x3 -> x0, blocking collectives: 112 us -> none
    unnamed x26 -> x0, waiting for transfers between devices: 101 us -> none
    unnamed x273 -> x27, local copies, waits for them, and re-layouts: 39.8 us -> 5.92 us
  transfers between devices with their start and end apart: 22 -> 2, of which waited for: 17 -> 0; matrix products, arithmetic and copies ran while one was open for 10% -> 4% of each run, Pallas kernels for 0% -> 58%
where the time goes in v1:
time: 356 us; the launch traced here: 355 us
  Pallas kernels  327 us (92%)
  local copies, waits for them, and re-layouts  16.7 us (5%)
  other arithmetic  7.09 us (2%)
  starting transfers between devices  3.56 us (1%)
    pallas_call x1, Pallas kernels, middle(): pl.pallas_call(middle_kernel, out_shape=[shape((slots, half, width), bf16...  122 us
    pallas_call x1, Pallas kernels, scatter_all(): pl.pallas_call(functools.partial(scatter_kernel, levels, parts), out_shap...  116 us
    pallas_call x1, Pallas kernels, gather_all(): pl.pallas_call(functools.partial(gather_kernel, levels, parts, late), out...  88.7 us
  transfers between devices with their start and end apart: 2, of which 0 were waited for; matrix products, arithmetic and copies ran while one was open for 4% of the time, Pallas kernels for 58%

profile of v1, /device:TPU:0, one launch (start us, length us, event | category | flops | bytes accessed | tf_op | source)
XLA Modules:
  0.0 354.9 jit_solution(12581719236755216794)
XLA Ops:
  0.7 0.0 copy-start.8
  0.7 3.0 collective-permute-start
  3.7 2.9 concatenate.7
  6.6 1.3 pad_add_fusion.refs_6_
  7.9 88.7 %gather_weights.1 = (bf16[32,24,768]{2,1,0:T(8,128)(2,1)}, bf16[32,24,768]{2,1,0:T(8,128)(2,1)}, bf16[32,24,768]{2,1,0:T(8,128)(2,1)}, bf16[32,24,768]{2,1,0:T(8...) custom-call(bf16[24,768]{1,0:T(8,128)(2,1)} %refs_0_.1, ...), custom_call_target="tpu_custom_call" | custom-call | tf_op jit(solution)/shard_map/gather_weights/pallas_call | solution.py:251
  96.6 1.0 convert_bitcast_fusion
  97.6 0.3 copy.41
  97.9 0.9 reshape.169.vec_ref
  98.8 0.9 convert_reduce_fusion
  99.7 0.7 reshape.170.inner_bias_ref
  100.4 0.0 copy-done.8
  100.5 0.7 compare_select_fusion.mask_ref
  101.1 0.0 collective-permute-done.other_ref
  101.1 0.0 copy-start.9
  101.1 0.9 copy-done.9
  102.0 122.2 %layer.1 = (bf16[2,256,768]{2,1,0:T(8,128)(2,1)}, f32[2,256,768]{2,1,0:T(8,128)}, bf16[2,256,768]{2,1,0:T(8,128)(2,1)}, f32[32,768]{1,0:T(8,128)}, f32[1,3072]{1...) custom-call(s32[2]{0:T(128)} %bitcast.78, ...), custom_call_target="tpu_custom_call" | custom-call | flops 31000000512 | bytes 40000000 | tf_op jit(solution)/shard_map/layer/pallas_call | solution.py:919
  224.2 1.3 reshape.168
  225.5 0.1 copy.44
  225.6 0.5 broadcast.63
  226.1 1.4 reduce.7
  227.5 0.1 reshape.167
  227.6 0.5 collective-permute-start.1
  228.2 0.8 select_convert_fusion.refs_6_
  229.0 0.0 copy-start
  229.0 115.9 %scatter_grads.1 = (f32[24,768]{1,0:T(8,128)}, f32[24,768]{1,0:T(8,128)}, f32[24,768]{1,0:T(8,128)}, f32[24,768]{1,0:T(8,128)}, f32[24,3072]{1,0:T(8,128)}, /*index=5*/f32[96,768]{1,0:T(8,128)}, f32[32,128]{1,0:T(8,128)}) custom-call(bf16[32,24,768]{2,1,0:T(8,128)(2,1)} %bitcast.53, bf16[32,24,768]{2,1,0:T(8,128)(2,1)} %bitcast.54, ...), custom_call_target="tpu_custom_call" | custom-call | tf_op jit(solution)/shard_map/scatter_grads/pallas_call | solution.py:472
  344.9 1.2 slice_bitcast_fusion.3
  346.1 1.4 slice_bitcast_fusion
  347.4 1.4 fusion.1
  348.8 0.0 collective-permute-done.1
  348.8 0.0 copy-done
  348.8 0.0 copy-start.1
  348.8 1.0 fusion
  349.9 0.0 copy-start.7
  349.9 0.0 copy-start.6
  349.9 0.0 copy-start.5
  349.9 0.0 copy-start.4
  349.9 0.0 copy-start.3
  349.9 0.0 copy-start.2
  349.9 0.2 copy-done.1
  350.1 0.9 copy.52
  350.9 0.0 copy-done.7
  350.9 0.6 copy.53
  351.6 0.0 copy-done.6
  351.6 0.6 copy.54
  352.2 0.0 copy-done.5
  352.2 0.6 copy.55
  352.8 0.0 copy-done.4
  352.8 0.6 copy.56
  353.5 0.0 copy-done.3
  353.5 0.7 copy.57
  354.2 0.0 copy-done.2
  354.2 0.7 copy.58
  (4 shorter events, 0.0 us)
Async XLA Ops:
  0.7 99.8 %copy-start.8 = (s32[1,2]{1,0:T(1,128)S(1)}, s32[1,2]{1,0:T(1,128)}, u32[]{:S(2)}) copy-start(s32[1,2]{1,0:T(1,128)} %param.24) | copy-start | bytes 28
  0.7 100.5 %collective-permute-start = (bf16[2,256,768]{2,1,0:T(8,128)(2,1)}, bf16[2,256,768]{2,1,0:T(8,128)(2,1)S(1)}, u32[]{:S(2)}, u32[]{:S(2)}) collective-permute-start(bf16[2,256,768]{2,1,0:T(8,128)(2,1)} %bitcast.75), channel_id=1, source_target_pairs={{0,16},{16,0},{1,17},{17,1},{2,18},{18,2},{3,19},{19,3},{4,20},{20... | collective-permute-start | bytes 2359304 | tf_op jit(solution)/shard_map/ppermute | solution.py:1021
  101.1 0.9 copy-start.9
  227.6 121.2 %collective-permute-start.1 = (bf16[2,256,768]{2,1,0:T(8,128)(2,1)}, bf16[2,256,768]{2,1,0:T(8,128)(2,1)S(1)}, u32[]{:S(2)}, u32[]{:S(2)}) collective-permute-start(bf16[2,256,768]{2,1,0:T(8,128)(2,1)} %get-tuple-element.53), channel_id=1, source_target_pairs={{0,16},{16,0},{1,17},{17,1},{2,18},{18,2},{3,19},{19,3},{4,20},{20... | collective-permute-start | bytes 2359304 | tf_op jit(solution)/shard_map/ppermute | solution.py:1053
  229.0 119.8 %copy-start = (f32[2,256,768]{2,1,0:T(8,128)S(1)}, f32[2,256,768]{2,1,0:T(8,128)}, u32[]{:S(2)}) copy-start(f32[2,256,768]{2,1,0:T(8,128)} %get-tuple-element.52) | copy-start | bytes 4718596
  348.8 1.3 copy-start.1
  349.9 1.1 copy-start.7
  349.9 1.7 copy-start.6
  349.9 2.4 copy-start.5
  349.9 3.0 copy-start.4
  349.9 3.6 %copy-start.3 = (f32[24,3072]{1,0:T(8,128)S(1)}, f32[24,3072]{1,0:T(8,128)}, u32[]{:S(2)}) copy-start(f32[24,3072]{1,0:T(8,128)} %get-tuple-element.111) | copy-start | bytes 884740
  349.9 4.3 %copy-start.2 = (f32[96,768]{1,0:T(8,128)S(1)}, f32[96,768]{1,0:T(8,128)}, u32[]{:S(2)}) copy-start(f32[96,768]{1,0:T(8,128)} %get-tuple-element.113) | copy-start | bytes 884740

commit v2 on v1

--- a/solution.py
+++ b/solution.py
@@ -510,327 +510,345 @@
     return jnp.sum(rows.reshape(rows.shape[0] // 8, 8, rows.shape[1]), axis=0)
 
 
-TILE = 256
 CHUNK = 48
 MEMORY = 32
 LANES = 128
-
-
-def middle_kernel(
-    start_ref,
-    mask_ref,
-    token_ref,
-    other_ref,
-    cot_ref,
-    vec_ref,
-    inner_bias_ref,
-    query_hbm,
-    key_hbm,
-    value_hbm,
-    output_hbm,
-    inner_hbm,
-    outer_hbm,
-    layer_ref,
-    own_ref,
-    pair_ref,
-    small_ref,
-    inner_bias_grad_ref,
-    query_grad_hbm,
-    key_grad_hbm,
-    value_grad_hbm,
-    output_grad_hbm,
-    inner_grad_hbm,
-    outer_grad_hbm,
-    wq,
-    wk,
-    wv,
-    wo,
-    wi,
-    w2,
-    hid,
-    query,
-    key,
-    value,
-    probs,
-    mixed,
-    normed_one,
-    normed_two,
-    inverse_one,
-    inverse_two,
-    first_b,
-    slope,
-    active,
-    grad_two_b,
-    grad_one_b,
-    grad_mixed,
-    grad_query,
-    grad_key,
-    grad_value,
-    work,
-    memory,
-    send_rows,
-    recv_rows,
-    stage,
-    load_sems,
-    stage_sems,
-    pair_sems,
-):
-    slots, half, width = token_ref.shape
-    rows = half + MEMORY
-    keys = rows + half
-    hidden_width = wi.shape[1]
-    pairs = width // LANES
-    scale = 1.0 / math.sqrt(width // HEADS)
-    seq = lax.axis_index("seq")
-    chain = lax.axis_index("chain")
-    is_owner = seq == 0
-    barrier = pltpu.get_barrier_semaphore()
-    pl.semaphore_signal(barrier, inc=1, device_id=(1 - seq, chain), device_id_type=MESH)
-    loads = [
-        pltpu.make_async_copy(source, target, load_sems.at[i])
-        for i, (source, target) in enumerate(
-            (
-                (query_hbm, wq),
-                (key_hbm, wk),
-                (value_hbm, wv),
-                (output_hbm, wo),
-                (inner_hbm, wi),
-                (outer_hbm, w2),
-            )
-        )
-    ]
-    for load in loads:
-        load.start()
-    line = 2 * MEM
-
-    def vec(at):
-        return vec_ref[line + at : line + at + 1, :]
-
-    def vec_tile(at, index):
-        return vec_ref[line + at : line + at + 1, span(index, TILE)]
-
-    lane = lax.broadcasted_iota(jnp.int32, (1, LANES), 1)
-    low_half = lane < LANES // 2
-    mem_row = lax.broadcasted_iota(jnp.int32, (MEMORY, 1), 0)
-    tiles = width // TILE
-
-    def half_of(values, which, factor):
-        keep = low_half if which == 0 else jnp.logical_not(low_half)
-        return values * jnp.where(keep, factor, 0.0).astype(values.dtype)
-
-    def forward(slot):
-        query_rows = pl.ds(half, rows)
-        hid[slot, 0:half] = other_ref[slot]
-        hid[slot, half : 2 * half] = token_ref[slot]
-        initial = jnp.where(mem_row < line, vec_ref[0:MEMORY, :], 0.0)
+LINE = 2 * MEM
+
+
+class Layer:
+    def __init__(self, seq, refs):
+        self.seq = seq
+        self.__dict__.update(refs)
+        self.slots, self.half, self.width = self.cot.shape
+        self.rows = self.half + MEMORY
+        self.keys = self.rows + self.half
+        self.hidden = self.w_inner.shape[1]
+        self.pairs = self.width // LANES
+        self.scale = 1.0 / math.sqrt(self.width // HEADS)
+        lane = lax.broadcasted_iota(jnp.int32, (1, LANES), 1)
+        self.low = lane < LANES // 2
+        self.low_f = jnp.where(self.low, 1.0, 0.0)
+        self.low_b = self.low_f.astype(jnp.bfloat16)
+        self.high_f = 1.0 - self.low_f
+        self.high_b = self.high_f.astype(jnp.bfloat16)
+        self.mem_row = lax.broadcasted_iota(jnp.int32, (MEMORY, 1), 0)
+
+    def vec(self, at):
+        return self.vectors[LINE + at : LINE + at + 1, :]
+
+    def slot_rows(self, slot):
+        return pl.ds(slot * self.rows, self.rows)
+
+    def slot_keys(self, slot):
+        return pl.ds(slot * self.keys, self.keys)
+
+    def slot_queries(self, slot):
+        return pl.ds(slot * self.keys + self.half, self.rows)
+
+    def weight(self, at):
+        return self.w_attention.at[:, pl.ds(at * self.width, self.width)]
+
+    def set_memory(self, slot):
+        initial = jnp.where(self.mem_row < LINE, self.vectors[0:MEMORY, :], 0.0)
         if slot > 0:
-            second = work[half:rows].astype(jnp.bfloat16).astype(jnp.float32)
+            second = self.work[self.half : self.rows].astype(jnp.bfloat16).astype(jnp.float32)
             carried = pltpu.roll(second, MEMORY - MEM, 0)
         else:
             carried = jnp.zeros_like(initial)
-        restart = start_ref[slot] == 1
-        initial = jnp.where(jnp.logical_or(mem_row >= MEM, restart), initial, carried)
-        hid[slot, 2 * half : keys] = initial.astype(jnp.bfloat16)
+        restart = self.start[slot] == 1
+        initial = jnp.where(jnp.logical_or(self.mem_row >= MEM, restart), initial, carried)
+        base = slot * self.keys + 2 * self.half
+        self.hid[base : base + MEMORY] = initial.astype(jnp.bfloat16)
+
+    def project_query(self, slot):
+        out = dot_nn(self.hid[self.slot_queries(slot)], self.weight(0)[...]) + self.vec(0)
+        self.query[self.slot_rows(slot)] = out.astype(jnp.bfloat16)
+
+    def project_key(self, slot):
+        self.key[self.slot_keys(slot)] = dot_nn(self.hid[self.slot_keys(slot)], self.weight(1)[...]).astype(
+            jnp.bfloat16
+        )
+
+    def project_value(self, slot):
+        out = dot_nn(self.hid[self.slot_keys(slot)], self.weight(2)[...]) + self.vec(1)
+        self.value[self.slot_keys(slot)] = out.astype(jnp.bfloat16)
+
+    def attend(self, slot):
+        valid = self.mask[slot]
+        low_scaled = (self.low_f * self.scale).astype(jnp.bfloat16)
+        high_scaled = (self.high_f * self.scale).astype(jnp.bfloat16)
+        rows = self.rows
+        for p in range(self.pairs):
+            here = pl.ds(p * LANES, LANES)
+            query_pair = self.query[self.slot_rows(slot), here]
+            key_pair = self.key[self.slot_keys(slot), here]
+            value_pair = self.value[self.slot_keys(slot), here]
+            stacked = jnp.concatenate([query_pair * low_scaled, query_pair * high_scaled], axis=0)
+            scores = dot_nt(stacked, key_pair) + valid
+            raised = jnp.exp(scores - jnp.max(scores, axis=1, keepdims=True)).astype(jnp.bfloat16)
+            self.shares[slot * self.pairs + p] = raised
+            ones = jnp.ones((self.keys, LANES), jnp.bfloat16)
+            summed = dot_nn(raised, jnp.concatenate([value_pair, ones], axis=1))
+            inverse = 1.0 / summed[:, LANES:]
+            out = summed[:, :LANES] * inverse
+            self.inverse_total[self.slot_rows(slot), here] = jnp.where(self.low, inverse[:rows], inverse[rows:])
+            self.mixed[self.slot_rows(slot), here] = jnp.where(self.low, out[:rows], out[rows:]).astype(jnp.bfloat16)
+
+    def norm(self, slot, normed, inverse, gain_at, shift_at, rounded=None):
+        for r in range(self.rows // CHUNK):
+            here = pl.ds(r * CHUNK, CHUNK)
+            there = pl.ds(slot * self.rows + r * CHUNK, CHUNK)
+            z = self.work[here, :]
+            centred = z - jnp.mean(z, axis=1, keepdims=True)
+            inv = lax.rsqrt(jnp.mean(centred * centred, axis=1, keepdims=True) + EPS)
+            unit = centred * inv
+            normed[there] = unit.astype(jnp.bfloat16)
+            inverse[there] = inv
+            out = unit * self.vec(gain_at) + self.vec(shift_at)
+            self.work[here, :] = out
+            if rounded is not None:
+                rounded[there] = out.astype(jnp.bfloat16)
+
+    def branch(self, slot):
+        out = dot_nn(self.mixed[self.slot_rows(slot)], self.weight(3)[...]) + self.vec(2)
+        self.work[...] = out + self.hid[self.slot_queries(slot)].astype(jnp.float32)
+        self.norm(slot, self.normed_one, self.inverse_one, 3, 4, self.first_b)
+
+    def inner(self, slot, j):
+        here = span(j, self.width)
+        u = dot_nn(self.first_b[self.slot_rows(slot)], self.w_inner[:, here]) + self.inner_bias[:, here]
+        cumulative = 0.5 * (1.0 + lax.erf(u * INV_ROOT_TWO))
+        density = jnp.exp(-0.5 * u * u) * INV_ROOT_TWO_PI
+        self.active[self.slot_rows(slot), here] = (u * cumulative).astype(jnp.bfloat16)
+        self.slope[self.slot_rows(slot), here] = (cumulative + u * density).astype(jnp.bfloat16)
+
+    def outer(self, slot):
+        self.work[...] += dot_nn(self.active[self.slot_rows(slot)], self.w_outer[...]) + self.vec(5)
+        self.norm(slot, self.normed_two, self.inverse_two, 6, 7)
+        self.layer_out[slot] = self.work[0 : self.half].astype(jnp.bfloat16)
+
+    def add_small(self, at, folded):
+        self.small[LINE + at : LINE + at + 1, :] += jnp.sum(folded, axis=0, keepdims=True)
+
+    def norm_back(self, slot, normed, inverse, gain_at, shift_at, bias_at, rounded):
+        zero = jnp.zeros((8, self.width), jnp.float32)
+        gain_sum, shift_sum, bias_sum = zero, zero, zero
+        for r in range(self.rows // CHUNK):
+            here = pl.ds(r * CHUNK, CHUNK)
+            there = pl.ds(slot * self.rows + r * CHUNK, CHUNK)
+            grad = self.work[here, :]
+            unit = normed[there].astype(jnp.float32)
+            gain_sum = gain_sum + fold(grad * unit)
+            shift_sum = shift_sum + fold(grad)
+            scaled = grad * self.vec(gain_at)
+            dz = inverse[there] * (
+                scaled
+                - jnp.mean(scaled, axis=1, keepdims=True)
+                - unit * jnp.mean(scaled * unit, axis=1, keepdims=True)
+            )
+            self.work[here, :] = dz
+            dz_b = dz.astype(jnp.bfloat16)
+            rounded[there] = dz_b
+            bias_sum = bias_sum + fold(dz_b.astype(jnp.float32))
+        self.add_small(gain_at, gain_sum)
+        self.add_small(shift_at, shift_sum)
+        self.add_small(bias_at, bias_sum)
+
+    def outer_back(self, slot):
+        self.work[0 : self.half] = self.cot[slot].astype(jnp.float32)
+        self.work[self.half : self.rows] = self.memory[...]
+        self.norm_back(slot, self.normed_two, self.inverse_two, 6, 7, 5, self.grad_two_b)
+
+        def tile(j):
+            here = span(j, self.width)
+            rows = self.slot_rows(slot)
+            grad = dot_nt(self.grad_two_b[rows], self.w_outer[here, :]) * self.slope[rows, here].astype(jnp.float32)
+            grad_b = grad.astype(jnp.bfloat16)
+            self.slope[rows, here] = grad_b
+            self.inner_bias_grad[:, here] += jnp.sum(fold(grad_b.astype(jnp.float32)), axis=0, keepdims=True)
+
+        fori(self.hidden // self.width, tile)
+
+    def inner_back(self, slot):
+        self.work[...] += dot_nt(self.slope[self.slot_rows(slot)], self.w_inner[...])
+        self.norm_back(slot, self.normed_one, self.inverse_one, 3, 4, 2, self.grad_one_b)
+
+    def attend_back(self, slot):
+        rows = self.rows
+        own = self.slot_rows(slot)
+        every = self.slot_keys(slot)
+        self.grad_mixed[...] = dot_nt(self.grad_one_b[own], self.weight(3)[...])
+
+        def pair(p):
+            here = pl.ds(p * LANES, LANES)
+            query_pair = self.query[own, here]
+            key_pair = self.key[every, here]
+            value_pair = self.value[every, here]
+            grad = self.grad_mixed[:, here].astype(jnp.bfloat16).astype(jnp.float32) * self.inverse_total[own, here]
+            product = grad * self.mixed[own, here].astype(jnp.float32)
+            delta = jnp.concatenate(
+                [
+                    jnp.sum(product * self.low_f, axis=1, keepdims=True),
+                    jnp.sum(product * self.high_f, axis=1, keepdims=True),
+                ],
+                axis=0,
+            )
+            grad_b = grad.astype(jnp.bfloat16)
+            stacked = jnp.concatenate([grad_b * self.low_b, grad_b * self.high_b], axis=0)
+            raised = self.shares[slot * self.pairs + p]
+            grad_scores = (raised.astype(jnp.float32) * (dot_nt(stacked, value_pair) - delta)).astype(jnp.bfloat16)
+            both = dot_nn(grad_scores, key_pair)
+            query_b = (jnp.where(self.low, both[:rows], both[rows:]) * self.scale).astype(jnp.bfloat16)
+            queries = jnp.concatenate([query_pair * self.low_b, query_pair * self.high_b], axis=0)
+            value_b = dot_tn(stacked, raised).T.astype(jnp.bfloat16)
+            self.grad_query[own, here] = query_b
+            self.grad_key[every, here] = (dot_tn(queries, grad_scores) * self.scale).T.astype(jnp.bfloat16)
+            self.grad_value[every, here] = value_b
+            self.small[LINE : LINE + 1, here] += jnp.sum(fold(query_b.astype(jnp.float32)), axis=0, keepdims=True)
+            self.small[LINE + 1 : LINE + 2, here] += jnp.sum(fold(value_b.astype(jnp.float32)), axis=0, keepdims=True)
+
+        for p in range(self.pairs):
+            pair(p)
+
+    def input_back(self, slot):
+        every = self.slot_keys(slot)
+        half = self.half
+        grads = dot_nt(self.grad_key[every], self.weight(1)[...]) + dot_nt(self.grad_value[every], self.weight(2)[...])
+        self.pair_out[slot] = grads[0:half].astype(jnp.bfloat16)
+        mine = grads[half:] + dot_nt(self.grad_query[self.slot_rows(slot)], self.weight(0)[...]) + self.work[...]
+        self.own_out[slot] = mine[0:half]
+        memory = mine[half:]
+        restart = self.start[slot] == 1
+        counted = jnp.logical_or(
+            jnp.logical_and(self.mem_row < MEM, restart),
+            jnp.logical_and(self.mem_row >= MEM, self.mem_row < LINE),
+        )
+        self.small[0:MEMORY, :] += jnp.where(counted, memory, 0.0)
+        return jnp.where(jnp.logical_and(self.mem_row < MEM, jnp.logical_not(restart)), memory, 0.0)
+
+    def outer_weight_grad(self, j):
+        here = span(j, self.width)
+        self.w_outer[here, :] = dot_tn(self.active[:, here], self.grad_two_b[...]).astype(jnp.bfloat16)
+
+    def inner_weight_grad(self, j):
+        here = span(j, self.width)
+        self.w_inner[:, here] = dot_tn(self.first_b[...], self.slope[:, here]).astype(jnp.bfloat16)
+
+    def output_weight_grad(self):
+        self.weight(3)[...] = dot_tn(self.mixed[...], self.grad_one_b[...]).astype(jnp.bfloat16)
+
+    def query_weight_grad(self):
+        total = None
+        for slot in range(self.slots):
+            term = dot_tn(self.hid[self.slot_queries(slot)], self.grad_query[self.slot_rows(slot)])
+            total = term if total is None else total + term
+        self.weight(0)[...] = total.astype(jnp.bfloat16)
+
+    def key_weight_grad(self):
+        self.weight(1)[...] = dot_tn(self.hid[...], self.grad_key[...]).astype(jnp.bfloat16)
+
+    def value_weight_grad(self):
+        self.weight(2)[...] = dot_tn(self.hid[...], self.grad_value[...]).astype(jnp.bfloat16)
+
+
+def state_shapes(slots, half, width, hidden):
+    rows, keys = half + MEMORY, 2 * half + MEMORY
+    bf16, f32 = jnp.bfloat16, jnp.float32
+    pairs = width // LANES
+    return {
+        "w_attention": ((width, 4 * width), bf16),
+        "w_inner": ((width, hidden), bf16),
+        "w_outer": ((hidden, width), bf16),
+        "hid": ((slots * keys, width), bf16),
+        "query": ((slots * rows, width), bf16),
+        "key": ((slots * keys, width), bf16),
+        "value": ((slots * keys, width), bf16),
+        "shares": ((slots * pairs, 2 * rows, keys), bf16),
+        "inverse_total": ((slots * rows, width), f32),
+        "mixed": ((slots * rows, width), bf16),
+        "normed_one": ((slots * rows, width), bf16),
+        "normed_two": ((slots * rows, width), bf16),
+        "inverse_one": ((slots * rows, 1), f32),
+        "inverse_two": ((slots * rows, 1), f32),
+        "first_b": ((slots * rows, width), bf16),
+        "slope": ((slots * rows, hidden), bf16),
+        "active": ((slots * rows, hidden), bf16),
+        "grad_two_b": ((slots * rows, width), bf16),
+        "grad_one_b": ((slots * rows, width), bf16),
+        "grad_mixed": ((rows, width), f32),
+        "grad_query": ((slots * rows, width), bf16),
+        "grad_key": ((slots * keys, width), bf16),
+        "grad_value": ((slots * keys, width), bf16),
+        "work": ((rows, width), f32),
+        "memory": ((MEMORY, width), f32),
+        "swap_out": ((MEMORY, width), f32),
+        "swap_in": ((MEMORY, width), f32),
+    }
+
+
+INPUTS = ("start", "mask", "tokens", "others", "cot", "vectors", "inner_bias")
+OUTPUTS = ("layer_out", "own_out", "pair_out", "small", "inner_bias_grad")
+
+
+def middle_kernel(names, *refs):
+    refs = list(refs)
+    given = {name: refs.pop(0) for name in INPUTS}
+    weights = [refs.pop(0) for _ in range(6)]
+    given.update({name: refs.pop(0) for name in OUTPUTS})
+    grads = [refs.pop(0) for _ in range(6)]
+    given.update({name: refs.pop(0) for name in names})
+    load_sems, pair_sems = refs
+    seq = lax.axis_index("seq")
+    chain = lax.axis_index("chain")
+    barrier = pltpu.get_barrier_semaphore()
+    pl.semaphore_signal(barrier, inc=1, device_id=(1 - seq, chain), device_id_type=MESH)
+    layer = Layer(seq, given)
+    places = [layer.weight(i) for i in range(4)] + [layer.w_inner, layer.w_outer]
+    loads = [pltpu.make_async_copy(weights[i], places[i], load_sems.at[i]) for i in range(6)]
+    stores = [pltpu.make_async_copy(places[i], grads[i], load_sems.at[i]) for i in range(6)]
+    for load in loads:
+        load.start()
+    layer.small[...] = jnp.zeros_like(layer.small)
+    layer.inner_bias_grad[...] = jnp.zeros_like(layer.inner_bias_grad)
+    for slot in range(layer.slots):
+        def need(i):
+            if slot == 0:
+                loads[i].wait()
+        base = slot * layer.keys
+        layer.hid[base : base + layer.half] = layer.others[slot]
+        layer.hid[base + layer.half : base + 2 * layer.half] = layer.tokens[slot]
+        layer.set_memory(slot)
+        need(0)
+        layer.project_query(slot)
+        need(1)
+        layer.project_key(slot)
+        need(2)
+        layer.project_value(slot)
+        layer.attend(slot)
+        need(3)
+        layer.branch(slot)
+        need(4)
+        fori(layer.hidden // layer.width, lambda j: layer.inner(slot, j))
+        need(5)
+        layer.outer(slot)
+    layer.memory[...] = jnp.zeros_like(layer.memory)
+    for slot in reversed(range(layer.slots)):
+        layer.outer_back(slot)
+        layer.inner_back(slot)
         if slot == 0:
-            loads[0].wait()
-
-        def query_tile(j):
-            query[slot, :, span(j, TILE)] = (
-                dot_nn(hid[slot, query_rows], wq[:, span(j, TILE)]) + vec_tile(0, j)
-            ).astype(jnp.bfloat16)
-
-        fori(tiles, query_tile)
-        if slot == 0:
-            loads[1].wait()
-
-        def key_tile(j):
-            key[slot, :, span(j, TILE)] = dot_nn(hid[slot], wk[:, span(j, TILE)]).astype(jnp.bfloat16)
-
-        fori(tiles, key_tile)
-        if slot == 0:
-            loads[2].wait()
-
-        def value_tile(j):
-            value[slot, :, span(j, TILE)] = (dot_nn(hid[slot], wv[:, span(j, TILE)]) + vec_tile(1, j)).astype(
-                jnp.bfloat16
-            )
-
-        fori(tiles, value_tile)
-        valid = mask_ref[slot]
-
-        def attend(p):
-            here = span(p, LANES)
-            query_pair = query[slot, :, here]
-            key_pair = key[slot, :, here]
-            value_pair = value[slot, :, here]
-            sides = []
-            for which in range(2):
-                scores = dot_nt(half_of(query_pair, which, scale), key_pair) + valid
-                top = jnp.max(scores, axis=1, keepdims=True)
-                raised = jnp.exp(scores - top)
-                total = jnp.sum(raised, axis=1, keepdims=True)
-                share = (raised * (1.0 / total)).astype(jnp.bfloat16)
-                probs[slot, 2 * p + which] = share
-                sides.append(dot_nn(share, value_pair))
-            mixed[slot, :, here] = jnp.where(low_half, sides[0], sides[1]).astype(jnp.bfloat16)
-
-        fori(pairs, attend)
-        if slot == 0:
-            loads[3].wait()
-
-        def branch_tile(j):
-            here = span(j, TILE)
-            work[:, here] = (
-                dot_nn(mixed[slot], wo[:, here]) + vec_tile(2, j) + hid[slot, query_rows, here].astype(jnp.float32)
-            )
-
-        fori(tiles, branch_tile)
-
-        def norm_chunk(normed, inverse, gain_at, shift_at):
-            def body(r):
-                here = span(r, CHUNK)
-                z = work[here, :]
-                centred = z - jnp.mean(z, axis=1, keepdims=True)
-                inv = lax.rsqrt(jnp.mean(centred * centred, axis=1, keepdims=True) + EPS)
-                unit = centred * inv
-                normed[slot, here] = unit.astype(jnp.bfloat16)
-                inverse[slot, here] = inv
-                out = unit * vec(gain_at) + vec(shift_at)
-                work[here, :] = out
-                if normed is normed_one:
-                    first_b[slot, here] = out.astype(jnp.bfloat16)
-
-            return body
-
-        fori(rows // CHUNK, norm_chunk(normed_one, inverse_one, 3, 4))
-        if slot == 0:
-            loads[4].wait()
-
-        def inner_tile(j):
-            here = span(j, TILE)
-            u = dot_nn(first_b[slot], wi[:, here]) + inner_bias_ref[:, here]
-            cumulative = 0.5 * (1.0 + lax.erf(u * INV_ROOT_TWO))
-            density = jnp.exp(-0.5 * u * u) * INV_ROOT_TWO_PI
-            active[slot, :, here] = (u * cumulative).astype(jnp.bfloat16)
-            slope[slot, :, here] = (cumulative + u * density).astype(jnp.bfloat16)
-
-        fori(hidden_width // TILE, inner_tile)
-        if slot == 0:
-            loads[5].wait()
-
-        def outer_tile(j):
-            here = span(j, TILE)
-            work[:, here] += dot_nn(active[slot], w2[:, here]) + vec_tile(5, j)
-
-        fori(tiles, outer_tile)
-        fori(rows // CHUNK, norm_chunk(normed_two, inverse_two, 6, 7))
-        layer_ref[slot] = work[0:half].astype(jnp.bfloat16)
-
-    def add_small(at, folded):
-        small_ref[line + at : line + at + 1, :] += jnp.sum(folded, axis=0, keepdims=True)
-
-    def backward(slot):
-        work[0:half] = cot_ref[slot].astype(jnp.float32)
-        work[half:rows] = memory[...]
-
-        def norm_back_pass(normed, inverse, gain_at, shift_at, bias_at, rounded):
-            zero = jnp.zeros((8, width), jnp.float32)
-
-            def body(r, sums):
-                here = span(r, CHUNK)
-                grad = work[here, :]
-                unit = normed[slot, here].astype(jnp.float32)
-                gain_sum = sums[0] + fold(grad * unit)
-                shift_sum = sums[1] + fold(grad)
-                scaled = grad * vec(gain_at)
-                dz = inverse[slot, here] * (
-                    scaled
-                    - jnp.mean(scaled, axis=1, keepdims=True)
-                    - unit * jnp.mean(scaled * unit, axis=1, keepdims=True)
-                )
-                work[here, :] = dz
-                dz_b = dz.astype(jnp.bfloat16)
-                rounded[slot, here] = dz_b
-                return (gain_sum, shift_sum, sums[2] + fold(dz_b.astype(jnp.float32)))
-
-            sums = lax.fori_loop(0, rows // CHUNK, body, (zero, zero, zero))
-            add_small(gain_at, sums[0])
-            add_small(shift_at, sums[1])
-            add_small(bias_at, sums[2])
-
-        norm_back_pass(normed_two, inverse_two, 6, 7, 5, grad_two_b)
-
-        def inner_tile(j):
-            here = span(j, TILE)
-            grad = (dot_nt(grad_two_b[slot], w2[here, :]) * slope[slot, :, here].astype(jnp.float32)).astype(
-                jnp.bfloat16
-            )
-            slope[slot, :, here] = grad
-            inner_bias_grad_ref[:, here] += jnp.sum(grad.astype(jnp.float32), axis=0, keepdims=True)
-
-        fori(hidden_width // TILE, inner_tile)
-
-        def first_tile(j):
-            here = span(j, TILE)
-            work[:, here] += dot_nt(slope[slot], wi[here, :])
-
-        fori(tiles, first_tile)
-        norm_back_pass(normed_one, inverse_one, 3, 4, 2, grad_one_b)
-
-        def mixed_tile(j):
-            here = span(j, TILE)
-            grad_mixed[:, here] = dot_nt(grad_one_b[slot], wo[here, :]).astype(jnp.bfloat16)
-
-        fori(tiles, mixed_tile)
-
-        def attend(p):
-            here = span(p, LANES)
-            query_pair = query[slot, :, here]
-            key_pair = key[slot, :, here]
-            value_pair = value[slot, :, here]
-            mixed_pair = grad_mixed[:, here]
-            dq, dk, dv = [], [], []
-            for which in range(2):
-                share = probs[slot, 2 * p + which]
-                grad = dot_nt(half_of(mixed_pair, which, 1.0), value_pair)
-                soft = share.astype(jnp.float32)
-                delta = jnp.sum(grad * soft, axis=1, keepdims=True)
-                grad_b = (soft * (grad - delta)).astype(jnp.bfloat16)
-                dq.append(dot_nn(grad_b, key_pair))
-                dk.append(dot_tn(grad_b, query_pair))
-                dv.append(dot_tn(share, mixed_pair))
-            dq_b = (jnp.where(low_half, dq[0], dq[1]) * scale).astype(jnp.bfloat16)
-            dv_b = jnp.where(low_half, dv[0], dv[1]).astype(jnp.bfloat16)
-            grad_query[slot, :, here] = dq_b
-            grad_key[slot, :, here] = (jnp.where(low_half, dk[0], dk[1]) * scale).astype(jnp.bfloat16)
-            grad_value[slot, :, here] = dv_b
-            small_ref[line : line + 1, here] += jnp.sum(dq_b.astype(jnp.float32), axis=0, keepdims=True)
-            small_ref[line + 1 : line + 2, here] += jnp.sum(dv_b.astype(jnp.float32), axis=0, keepdims=True)
-
-        fori(pairs, attend)
-
-        def input_tile(j):
-            here = span(j, TILE)
-            both = dot_nt(grad_key[slot], wk[here, :]) + dot_nt(grad_value[slot], wv[here, :])
-            pair_ref[slot, :, here] = both[0:half].astype(jnp.bfloat16)
-            mine = both[half:keys] + dot_nt(grad_query[slot], wq[here, :]) + work[:, here]
-            own_ref[slot, :, here] = mine[0:half]
-            memory[:, here] = mine[half:rows]
-
-        fori(tiles, input_tile)
-        restart = start_ref[slot] == 1
-        grads = memory[...]
-        counted = jnp.logical_or(
-            jnp.logical_and(mem_row < MEM, restart), jnp.logical_and(mem_row >= MEM, mem_row < line)
-        )
-        small_ref[0:MEMORY, :] += jnp.where(counted, grads, 0.0)
+            fori(layer.hidden // layer.width, layer.outer_weight_grad)
+            stores[5].start()
+            fori(layer.hidden // layer.width, layer.inner_weight_grad)
+            stores[4].start()
+        layer.attend_back(slot)
+        passed = layer.input_back(slot)
         if slot > 0:
-            passed = jnp.where(jnp.logical_and(mem_row < MEM, jnp.logical_not(restart)), grads, 0.0)
-            send_rows[...] = passed
+            layer.swap_out[...] = passed
             pl.semaphore_wait(barrier, 1)
             swap = pltpu.make_async_remote_copy(
-                src_ref=send_rows,
-                dst_ref=recv_rows,
+                src_ref=layer.swap_out,
+                dst_ref=layer.swap_in,
                 send_sem=pair_sems.at[0],
                 recv_sem=pair_sems.at[1],
                 device_id=(1 - seq, chain),
@@ -838,126 +856,42 @@
             )
             swap.start()
             swap.wait()
-            summed = pltpu.roll(passed + recv_rows[...], MEM, 0)
-            memory[...] = jnp.where(is_owner, summed, 0.0)
-
-    small_ref[...] = jnp.zeros_like(small_ref)
-    inner_bias_grad_ref[...] = jnp.zeros_like(inner_bias_grad_ref)
-    for slot in range(slots):
-        forward(slot)
-    memory[...] = jnp.zeros_like(memory)
-    for slot in reversed(range(slots)):
-        backward(slot)
-
-    def emit(count, compute, target):
-        def copy(j):
-            buffer = lax.rem(j, 2)
-            return pltpu.make_async_copy(stage.at[buffer], target(j), stage_sems.at[buffer])
-
-        def body(j):
-            @pl.when(j >= 2)
-            def _():
-                copy(j - 2).wait()
-
-            stage[lax.rem(j, 2)] = compute(j).astype(jnp.bfloat16)
-            copy(j).start()
-
-        fori(count, body)
-        copy(count - 2).wait()
-        copy(count - 1).wait()
-
-    def product(former, latter):
-        total = None
-        for slot in range(slots):
-            term = dot_tn(former(slot), latter(slot))
-            total = term if total is None else total + term
-        return total
-
-    emit(
-        tiles,
-        lambda j: product(lambda s: hid[s, half:keys, span(j, TILE)], lambda s: grad_query[s]),
-        lambda j: query_grad_hbm.at[span(j, TILE)],
-    )
-    emit(
-        tiles,
-        lambda j: product(lambda s: hid[s, :, span(j, TILE)], lambda s: grad_key[s]),
-        lambda j: key_grad_hbm.at[span(j, TILE)],
-    )
-    emit(
-        tiles,
-        lambda j: product(lambda s: hid[s, :, span(j, TILE)], lambda s: grad_value[s]),
-        lambda j: value_grad_hbm.at[span(j, TILE)],
-    )
-    emit(
-        tiles,
-        lambda j: product(lambda s: mixed[s, :, span(j, TILE)], lambda s: grad_one_b[s]),
-        lambda j: output_grad_hbm.at[span(j, TILE)],
-    )
-    emit(
-        hidden_width // TILE,
-        lambda j: product(
-            lambda s: first_b[s, :, span(lax.rem(j, tiles), TILE)], lambda s: slope[s, :, span(j // tiles, width)]
-        ),
-        lambda j: inner_grad_hbm.at[span(lax.rem(j, tiles), TILE), span(j // tiles, width)],
-    )
-    emit(
-        hidden_width // TILE,
-        lambda j: product(lambda s: active[s, :, span(j, TILE)], lambda s: grad_two_b[s]),
-        lambda j: outer_grad_hbm.at[span(j, TILE)],
-    )
+            summed = pltpu.roll(passed + layer.swap_in[...], MEM, 0)
+            layer.memory[...] = jnp.where(seq == 0, summed, 0.0)
+    layer.output_weight_grad()
+    stores[3].start()
+    layer.query_weight_grad()
+    stores[0].start()
+    layer.key_weight_grad()
+    stores[1].start()
+    layer.value_weight_grad()
+    stores[2].start()
+    for store in stores:
+        store.wait()
 
 
 def middle(start, mask, tokens, others, cotangent, vectors, inner_bias, weights):
     slots, half, width = tokens.shape
-    rows, keys = half + MEMORY, 2 * half + MEMORY
-    hidden_width = inner_bias.shape[1]
+    hidden = inner_bias.shape[1]
     bf16, f32 = jnp.bfloat16, jnp.float32
     inside = pl.BlockSpec(memory_space=pltpu.VMEM)
     anywhere = pl.BlockSpec(memory_space=pl.ANY)
     shape = jax.ShapeDtypeStruct
-    dma = pltpu.SemaphoreType.DMA
+    state = state_shapes(slots, half, width, hidden)
     return pl.pallas_call(
-        middle_kernel,
+        functools.partial(middle_kernel, tuple(state)),
         out_shape=[
             shape((slots, half, width), bf16),
             shape((slots, half, width), f32),
             shape((slots, half, width), bf16),
             shape((MEMORY, width), f32),
-            shape((1, hidden_width), f32),
+            shape((1, hidden), f32),
         ]
         + [shape(w.shape, bf16) for w in weights],
         in_specs=[pl.BlockSpec(memory_space=pltpu.SMEM)] + [inside] * 6 + [anywhere] * 6,
         out_specs=[inside] * 5 + [anywhere] * 6,
-        scratch_shapes=[pltpu.VMEM(w.shape, bf16) for w in weights]
-        + [
-            pltpu.VMEM((slots, keys, width), bf16),
-            pltpu.VMEM((slots, rows, width), bf16),
-            pltpu.VMEM((slots, keys, width), bf16),
-            pltpu.VMEM((slots, keys, width), bf16),
-            pltpu.VMEM((slots, HEADS, rows, keys), bf16),
-            pltpu.VMEM((slots, rows, width), bf16),
-            pltpu.VMEM((slots, rows, width), bf16),
-            pltpu.VMEM((slots, rows, width), bf16),
-            pltpu.VMEM((slots, rows, 1), f32),
-            pltpu.VMEM((slots, rows, 1), f32),
-            pltpu.VMEM((slots, rows, width), bf16),
-            pltpu.VMEM((slots, rows, hidden_width), bf16),
-            pltpu.VMEM((slots, rows, hidden_width), bf16),
-            pltpu.VMEM((slots, rows, width), bf16),
-            pltpu.VMEM((slots, rows, width), bf16),
-            pltpu.VMEM((rows, width), bf16),
-            pltpu.VMEM((slots, rows, width), bf16),
-            pltpu.VMEM((slots, keys, width), bf16),
-            pltpu.VMEM((slots, keys, width), bf16),
-            pltpu.VMEM((rows, width), f32),
-            pltpu.VMEM((MEMORY, width), f32),
-            pltpu.VMEM((MEMORY, width), f32),
-            pltpu.VMEM((MEMORY, width), f32),
-            pltpu.VMEM((2, TILE, width), bf16),
-            dma((6,)),
-            dma((2,)),
-            dma((2,)),
-        ],
+        scratch_shapes=[pltpu.VMEM(*s) for s in state.values()]
+        + [pltpu.SemaphoreType.DMA((6,)), pltpu.SemaphoreType.DMA((2,))],
         compiler_params=pltpu.CompilerParams(
             collective_id=2, has_side_effects=True, vmem_limit_bytes=62 * 2**20
         ),

time: 356 us -> 313 us (0.88)
  Pallas kernels: 327 us -> 280 us
    pallas_call x1, Pallas kernels: 122 us -> 75 us  [middle(): pl.pallas_call(functools.partial(middle_kernel, tuple(state)), out_shape=...]
  transfers between devices with their start and end apart: 2 -> 2, of which waited for: 0 -> 0; matrix products, arithmetic and copies ran while one was open for 4% -> 4% of each run, Pallas kernels for 58% -> 67%
where the time goes in v2:
time: 313 us; the launch traced here: 308 us
  Pallas kernels  280 us (89%)
  local copies, waits for them, and re-layouts  16.7 us (5%)
  other arithmetic  7.09 us (2%)
  starting transfers between devices  3.55 us (1%)
    pallas_call x1, Pallas kernels, scatter_all(): pl.pallas_call(functools.partial(scatter_kernel, levels, parts), out_shap...  116 us
    pallas_call x1, Pallas kernels, gather_all(): pl.pallas_call(functools.partial(gather_kernel, levels, parts, late), out...  89.1 us
    pallas_call x1, Pallas kernels, middle(): pl.pallas_call(functools.partial(middle_kernel, tuple(state)), out_shape=...  75 us
  transfers between devices with their start and end apart: 2, of which 0 were waited for; matrix products, arithmetic and copies ran while one was open for 4% of the time, Pallas kernels for 67%

profile of v2, /device:TPU:0, one launch (start us, length us, event | category | flops | bytes accessed | tf_op | source)
XLA Modules:
  0.0 308.4 jit_solution(3693025801201954865)
XLA Ops:
  0.7 0.0 copy-start.8
  0.7 3.0 collective-permute-start
  3.7 2.9 concatenate.7
  6.6 1.3 pad_add_fusion.refs_6_
  7.9 89.1 %gather_weights.1 = (bf16[32,24,768]{2,1,0:T(8,128)(2,1)}, bf16[32,24,768]{2,1,0:T(8,128)(2,1)}, bf16[32,24,768]{2,1,0:T(8,128)(2,1)}, bf16[32,24,768]{2,1,0:T(8...) custom-call(bf16[24,768]{1,0:T(8,128)(2,1)} %refs_0_.1, ...), custom_call_target="tpu_custom_call" | custom-call | tf_op jit(solution)/shard_map/gather_weights/pallas_call | solution.py:251
  97.0 1.0 convert_bitcast_fusion
  98.0 0.3 copy.41
  98.4 0.9 reshape.169.refs_5_
  99.3 0.9 convert_reduce_fusion
  100.2 0.7 reshape.170.refs_6_
  100.9 0.0 copy-done.8
  100.9 0.7 compare_select_fusion.refs_1_
  101.6 0.0 collective-permute-done.refs_3_
  101.6 0.0 copy-start.9
  101.6 0.9 copy-done.9
  102.5 75.0 %layer.1 = (bf16[2,256,768]{2,1,0:T(8,128)(2,1)}, f32[2,256,768]{2,1,0:T(8,128)}, bf16[2,256,768]{2,1,0:T(8,128)(2,1)}, f32[32,768]{1,0:T(8,128)}, f32[1,3072]{1...) custom-call(s32[2]{0:T(128)} %bitcast.78, ...), custom_call_target="tpu_custom_call" | custom-call | flops 31000000512 | bytes 40000000 | tf_op jit(solution)/shard_map/layer/pallas_call | solution.py:881
  177.5 1.3 reshape.168
  178.7 0.1 copy.44
  178.8 0.5 broadcast.63
  179.4 1.4 reduce.7
  180.7 0.1 reshape.167
  180.8 0.5 collective-permute-start.1
  181.4 0.8 select_convert_fusion.refs_6_
  182.2 0.0 copy-start
  182.2 116.0 %scatter_grads.1 = (f32[24,768]{1,0:T(8,128)}, f32[24,768]{1,0:T(8,128)}, f32[24,768]{1,0:T(8,128)}, f32[24,768]{1,0:T(8,128)}, f32[24,3072]{1,0:T(8,128)}, /*index=5*/f32[96,768]{1,0:T(8,128)}, f32[32,128]{1,0:T(8,128)}) custom-call(bf16[32,24,768]{2,1,0:T(8,128)(2,1)} %bitcast.53, bf16[32,24,768]{2,1,0:T(8,128)(2,1)} %bitcast.54, ...), custom_call_target="tpu_custom_call" | custom-call | tf_op jit(solution)/shard_map/scatter_grads/pallas_call | solution.py:472
  298.1 1.2 slice_bitcast_fusion.3
  299.3 1.4 slice_bitcast_fusion
  300.7 1.4 fusion.1
  302.1 0.0 collective-permute-done.1
  302.1 0.0 copy-done
  302.1 0.0 copy-start.1
  302.1 1.0 fusion
  303.1 0.0 copy-start.7
  303.1 0.0 copy-start.6
  303.1 0.0 copy-start.5
  303.1 0.0 copy-start.4
  303.1 0.0 copy-start.3
  303.1 0.0 copy-start.2
  303.1 0.2 copy-done.1
  303.3 0.9 copy.52
  304.2 0.0 copy-done.7
  304.2 0.6 copy.53
  304.8 0.0 copy-done.6
  304.8 0.6 copy.54
  305.5 0.0 copy-done.5
  305.5 0.6 copy.55
  306.1 0.0 copy-done.4
  306.1 0.6 copy.56
  306.7 0.0 copy-done.3
  306.7 0.7 copy.57
  307.5 0.0 copy-done.2
  307.5 0.7 copy.58
  (4 shorter events, 0.0 us)
Async XLA Ops:
  0.7 100.2 %copy-start.8 = (s32[1,2]{1,0:T(1,128)S(1)}, s32[1,2]{1,0:T(1,128)}, u32[]{:S(2)}) copy-start(s32[1,2]{1,0:T(1,128)} %param.24) | copy-start | bytes 28
  0.7 100.9 %collective-permute-start = (bf16[2,256,768]{2,1,0:T(8,128)(2,1)}, bf16[2,256,768]{2,1,0:T(8,128)(2,1)S(1)}, u32[]{:S(2)}, u32[]{:S(2)}) collective-permute-start(bf16[2,256,768]{2,1,0:T(8,128)(2,1)} %bitcast.75), channel_id=1, source_target_pairs={{0,16},{16,0},{1,17},{17,1},{2,18},{18,2},{3,19},{19,3},{4,20},{20... | collective-permute-start | bytes 2359304 | tf_op jit(solution)/shard_map/ppermute | solution.py:955
  101.6 0.9 copy-start.9
  180.8 121.2 %collective-permute-start.1 = (bf16[2,256,768]{2,1,0:T(8,128)(2,1)}, bf16[2,256,768]{2,1,0:T(8,128)(2,1)S(1)}, u32[]{:S(2)}, u32[]{:S(2)}) collective-permute-start(bf16[2,256,768]{2,1,0:T(8,128)(2,1)} %get-tuple-element.53), channel_id=1, source_target_pairs={{0,16},{16,0},{1,17},{17,1},{2,18},{18,2},{3,19},{19,3},{4,20},{20... | collective-permute-start | bytes 2359304 | tf_op jit(solution)/shard_map/ppermute | solution.py:987
  182.2 119.9 %copy-start = (f32[2,256,768]{2,1,0:T(8,128)S(1)}, f32[2,256,768]{2,1,0:T(8,128)}, u32[]{:S(2)}) copy-start(f32[2,256,768]{2,1,0:T(8,128)} %get-tuple-element.52) | copy-start | bytes 4718596
  302.1 1.3 copy-start.1
  303.1 1.1 copy-start.7
  303.1 1.7 copy-start.6
  303.1 2.4 copy-start.5
  303.1 3.0 copy-start.4
  303.1 3.6 %copy-start.3 = (f32[24,3072]{1,0:T(8,128)S(1)}, f32[24,3072]{1,0:T(8,128)}, u32[]{:S(2)}) copy-start(f32[24,3072]{1,0:T(8,128)} %get-tuple-element.111) | copy-start | bytes 884740
  303.1 4.3 %copy-start.2 = (f32[96,768]{1,0:T(8,128)S(1)}, f32[96,768]{1,0:T(8,128)}, u32[]{:S(2)}) copy-start(f32[96,768]{1,0:T(8,128)} %get-tuple-element.113) | copy-start | bytes 884740
